TPU v7x, 512 devices: a whole 4x4x16 slice. The times are simulated.
512 devices in a mesh: tok: 32 (over z, core), batch: 16 (over y, x).
Axes of the slice: x: 4, y: 4, z: 16, core: 2. Of those that a mesh axis runs over, the one named last changes fastest.
Arguments:
- table: bfloat16 [524288, 256], P(('tok', 'batch')), may hold values from -6 to 6
- hist_owner: int32 [2048, 128, 1], P(('batch', 'tok')), may hold values from 0 to 511; in each aligned block of 512 rows (0 to 511, 512 to 1023, ..., all dimensions but the last counted through in order) at most 2 rows name the same one
- hist_row: int32 [2048, 128], P(('batch', 'tok')), may hold values from 0 to 1023
- hist_len: int32 [2048], P(('batch', 'tok')), may hold values from 1 to 128, 131072 in all
- w_in: bfloat16 [256, 1024], replicated, may hold values from -0.375 to 0.375
- queries: bfloat16 [64, 1024], replicated, may hold values from -1200 to 1200
- ffn_gain: float32 [64, 1024], P('tok'), may hold values from 0.1 to 1.9
- w_gate: bfloat16 [64, 1024, 768], P('tok', 'batch'), may hold values from -0.1875 to 0.1875
- w_up: bfloat16 [64, 1024, 768], P('tok', 'batch'), may hold values from -0.1875 to 0.1875
- w_down: bfloat16 [64, 768, 1024], P('tok', 'batch'), may hold values from -0.21875 to 0.21875
Outputs:
- tokens_out: bfloat16 [2048, 64, 1024], P('batch', 'tok')
Inputs may be any that keep to these rules, and one draw needn't show every extreme that they name: `hist_owner`: among the 512 slots of the users of one device, no owner is named more than 2 times, a bound that some block reaches.
All inputs are finite; a program needn't handle non-finite values. No bound on the sum of `hist_len` on one device may be relied on, other than what follows from the above.
Results may differ from a plain program's by a relative error of at most 0.019.
The roundings to bfloat16 on the way count: a program that leaves them out, or rounds other values in their place, can miss the bound.
Values may be sent and summed in bfloat16 or wider, within the bound.
No kernel may reach another device: no remote copies, remote signals or barrier semaphores. Data moves between devices by JAX's collectives and lax.ppermute only.
A program may use at most 64 MiB of HBM per device.

v0:
```python
import jax
import jax.numpy as jnp
from jax import lax
from jax.sharding import PartitionSpec as P


def rms_scale(values):
    return lax.rsqrt(jnp.mean(values * values, axis=-1, keepdims=True) + 1e-06)


def shards(table, hist_owner, hist_row, hist_len, w_in, queries, ffn_gain, w_gate, w_up, w_down):
    ntok = lax.axis_size("tok")
    nbatch = lax.axis_size("batch")
    devices = ntok * nbatch
    users = hist_row.shape[0]
    slots_user = hist_row.shape[1]
    emb = table.shape[1]
    width = w_in.shape[1]
    nquery = queries.shape[0]
    headsz = width // nquery
    count = users * slots_user
    capacity = 2 * count // devices
    owners = hist_owner.reshape(count)
    order = jnp.argsort(owners, stable=True)
    sorted_owner = owners[order]
    tallies = jnp.sum(
        (owners[:, None] == jnp.arange(devices, dtype=jnp.int32)[None, :]).astype(jnp.int32), axis=0
    )
    starts = jnp.cumsum(tallies) - tallies
    rank_sorted = jnp.arange(count, dtype=jnp.int32) - starts[sorted_owner]
    rank = jnp.zeros((count,), jnp.int32).at[order].set(rank_sorted)
    position = owners * capacity + rank
    request = jnp.zeros((devices * capacity,), jnp.int32).at[position].set(hist_row.reshape(count))
    request = request.reshape(ntok, nbatch, capacity)
    received = lax.all_to_all(
        lax.all_to_all(request, "tok", split_axis=0, concat_axis=0, tiled=True),
        "batch",
        split_axis=1,
        concat_axis=1,
        tiled=True,
    )
    served = jnp.take(table, received.reshape(-1), axis=0).reshape(ntok, nbatch, capacity, emb)
    answers = lax.all_to_all(
        lax.all_to_all(served, "tok", split_axis=0, concat_axis=0, tiled=True),
        "batch",
        split_axis=1,
        concat_axis=1,
        tiled=True,
    )
    rows = jnp.take(answers.reshape(devices * capacity, emb), position, axis=0)
    proj = jnp.dot(rows, w_in, preferred_element_type=jnp.float32)
    keys = (proj * rms_scale(proj)).astype(jnp.bfloat16).reshape(users, slots_user, nquery, headsz)
    query_heads = queries.reshape(nquery, nquery, headsz)
    root = jnp.sqrt(jnp.float32(headsz))

    def attend(args):
        key_user, len_user = args
        scores = (
            jnp.einsum("qhe,jhe->qhj", query_heads, key_user, preferred_element_type=jnp.float32)
            / root
        )
        valid = jnp.arange(slots_user) < len_user
        scores = jnp.where(valid[None, None, :], scores, jnp.float32(-1e30))
        attn = jax.nn.softmax(scores, axis=-1).astype(jnp.bfloat16)
        pooled_user = jnp.einsum("qhj,jhe->qhe", attn, key_user, preferred_element_type=jnp.float32)
        return pooled_user.astype(jnp.bfloat16).reshape(nquery, width)

    pooled = lax.map(attend, (keys, hist_len))
    regrouped = lax.all_to_all(pooled, "tok", split_axis=1, concat_axis=0, tiled=True)
    group = regrouped.shape[0]
    split_heads = regrouped.reshape(group, nquery // ntok, nquery, headsz)
    moved = lax.all_to_all(split_heads, "tok", split_axis=2, concat_axis=1, tiled=True)
    mixed = moved.transpose(0, 2, 1, 3).reshape(group, nquery // ntok, width)
    mixed_wide = mixed.astype(jnp.float32)
    normed = (mixed_wide * rms_scale(mixed_wide) * ffn_gain[None, :, :]).astype(jnp.bfloat16)
    local_tok = mixed.shape[1]

    def add_rows(piece):
        return jnp.einsum("uhd,hdf->huf", normed, piece, preferred_element_type=jnp.float32)

    gate = add_rows(lax.all_gather(w_gate, "batch", axis=1, tiled=True))
    up_val = add_rows(lax.all_gather(w_up, "batch", axis=1, tiled=True))
    hidden = (jax.nn.silu(gate) * up_val).astype(jnp.bfloat16)
    down = jnp.einsum(
        "huf,hfd->uhd",
        hidden,
        lax.all_gather(w_down, "batch", axis=1, tiled=True),
        preferred_element_type=jnp.float32,
    )
    summed = (mixed_wide + down).astype(jnp.bfloat16)
    spread = summed.reshape(group, local_tok, nquery, headsz)
    back = lax.all_to_all(spread, "tok", split_axis=2, concat_axis=1, tiled=True)
    return back.transpose(0, 2, 1, 3).reshape(group, nquery // ntok, width)


def solution(mesh):
    placed = (
        P(("tok", "batch"), None),
        P(("batch", "tok"), None, None),
        P(("batch", "tok"), None),
        P(("batch", "tok")),
        P(),
        P(),
        P("tok", None),
        P("tok", "batch", None),
        P("tok", "batch", None),
        P("tok", "batch", None),
    )
    return jax.shard_map(
        shards, mesh=mesh, in_specs=placed, out_specs=P("batch", "tok", None), check_vma=False
    )
```

profile of v0, /device:TPU:1, one launch (start us, length us, event | category | flops | bytes accessed | tf_op | source)
XLA Modules:
  0.0 296.0 jit_solution(14779168986544895904)
XLA Ops:
  9.3 4.4 %sort.17 = (s32[512]{0:T(512)}, s32[512]{0:T(512)S(1)}) sort(s32[512]{0:T(512)} %bitcast.75, s32[512]{0:T(512)S(1)} %iota.16), dimensions={0}, to_apply=%region_0.0 | sort | flops 4608 | bytes 8192 | tf_op jit(solution)/shard_map/jit(argsort)/sort | solution.py:24
  13.8 3.7 %gather_fusion = s32[512]{0:T(512)S(1)} fusion(s32[512]{0:T(512)} %bitcast.76, s32[1024]{0:T(1024)S(1)} %pad_clamp_fusion.2), kind=kCustom, calls=%fused_computation | custom fusion | bytes 6144 | tf_op jit(solution)/shard_map/gather | solution.py:25
  17.7 3.5 %gather_fusion.1 = s32[512]{0:T(512)S(1)} fusion(s32[512]{0:T(512)S(1)} %bitcast_subtract_fusion.1, s32[1024]{0:T(1024)S(1)} %pad_clamp_fusion.1), kind=kCustom, calls=%fused_computation.1 | custom fusion | bytes 6144 | tf_op jit(solution)/shard_map/gather | solution.py:30
  21.2 2.4 scatter_custom_fusion
  23.6 2.6 scatter_custom_fusion.1
  26.7 28.7 %all_to_all.65 = s32[32,16,2]{1,2,0:T(2,128)S(1)} all-to-all(s32[32,16,2]{1,2,0:T(2,128)S(1)} %copy.83), channel_id=1, replica_groups=mesh['tok'=32,'batch'=16] {'tok'}, dimensions={0} | all-to-all | bytes 8192 | tf_op jit(solution)/shard_map/all_to_all | solution.py:36
  55.5 13.0 %all_to_all.66 = s32[32,16,2]{0,2,1:T(2,128)S(1)} all-to-all(s32[32,16,2]{0,2,1:T(2,128)S(1)} %copy.84), channel_id=1, replica_groups=mesh['tok'=32,'batch'=16] {'batch'}, dimensions={1} | all-to-all | bytes 8192 | tf_op jit(solution)/shard_map/all_to_all | solution.py:35
  68.9 3.9 %gather_fusion.2 = bf16[1024,256]{1,0:T(8,128)(2,1)S(1)} fusion(bf16[1024,256]{1,0:T(8,128)(2,1)S(1)} %copy-done.2, s32[1024]{0:T(1024)S(1)} %broadcast_clamp_fusion), kind=kCustom, calls=%fused_computation.2 | custom fusion | bytes 1052672 | tf_op jit(solution)/shard_map/jit(_take)/gather | solution.py:42
  73.3 1.0 broadcast_select_fusion
  74.3 38.7 %all_to_all.67 = bf16[32,16,2,256]{3,2,1,0:T(2,128)(2,1)S(1)} all-to-all(bf16[32,16,2,256]{3,2,1,0:T(2,128)(2,1)S(1)} %broadcast_select_fusion), channel_id=1, replica_groups=mesh['tok'=32,'batch'=16] {'tok'}, dimensions={0} | all-to-all | bytes 1048576 | tf_op jit(solution)/shard_map/all_to_all | solution.py:44
  113.0 1.3 copy.87
  114.3 3.6 %all-to-all-start.3 = ((bf16[32,16,2,256]{3,2,0,1:T(2,128)(2,1)}), bf16[32,16,2,256]{3,2,0,1:T(2,128)(2,1)S(1)}, u32[]{:S(2)}, u32[]{:S(2)}) async-start(bf16[32,16,2,256]{3,2,0,1:T(2,128)(2,1)} %copy.87), calls=%async_computation.3 | async-start | bytes 1048576 | tf_op jit(solution)/shard_map/all_to_all | solution.py:43
  118.9 9.6 %all-to-all-done.3 = bf16[32,16,2,256]{3,2,0,1:T(2,128)(2,1)S(1)} async-done(((bf16[32,16,2,256]{3,2,0,1:T(2,128)(2,1)}), bf16[32,16,2,256]{3,2,0,1:T(2,128)(2,1)S(1)}, u32[]{:S(2)}, u32[]{:S(2)}) %all-to-all-start.3) | async-done | bytes 524320 | tf_op jit(solution)/shard_map/all_to_all | solution.py:43
  129.2 2.0 gather_fusion.3
  133.1 23.5 %while.10 = (s32[]{:T(128)}, bf16[4,64,1024]{2,0,1:T(4,128)(2,1)S(1)}, bf16[4,128,64,16]{1,3,2,0:T(8,128)(2,1)S(1)}, s32[4]{0:T(128)S(1)}, bf16[64,64,16]{0,2,1:T(8,128)(2,1)S(1)}, /*index=5*/s32[]{:T(128)}, s32[]{:T(128)}) while((s32[]{:T(128)}, bf16[4,64,1024]{2,0,1:T(4,128)(2,1)S(1)}, bf16[4,128,64,16]{1,3,2,0:T(8,128)(2,1)S(1)}, ...), condition=%wide.region_10.11_spmd, body=%wide.region_7.10_spmd.sunk | while | flops 37814528 | bytes 9879913 | solution.py:68
  134.9 1.2 fusion.53
  137.3 1.7 dynamic_update_slice.5
  140.8 1.2 fusion.53
  141.9 0.9 convolution_convert_fusion.2
  143.1 1.7 dynamic_update_slice.5
  146.6 1.2 fusion.53
  149.0 1.7 dynamic_update_slice.5
  152.5 1.2 fusion.53
  154.9 1.7 dynamic_update_slice.5
  156.7 38.1 %all_to_all.68 = bf16[4,64,1024]{2,0,1:T(4,128)(2,1)S(1)} all-to-all(bf16[4,64,1024]{2,0,1:T(4,128)(2,1)S(1)} %get-tuple-element.34), channel_id=1, replica_groups=mesh['tok'=32,'batch'=16] {'tok'}, dimensions={1} | all-to-all | bytes 1048576 | tf_op jit(solution)/shard_map/all_to_all | solution.py:69
  195.3 4.1 %reshape.145 = bf16[128,2,64,16]{3,2,1,0:T(8,128)(2,1)} reshape(bf16[32,4,2,1024]{3,2,1,0:T(2,128)(2,1)S(1)} %copy.93) | data formatting | bytes 1048576 | tf_op jit(solution)/shard_map/reshape | solution.py:71
  199.5 5.5 %copy.94 = bf16[128,2,64,16]{0,3,1,2:T(8,128)(2,1)S(1)} copy(bf16[128,2,64,16]{3,2,1,0:T(8,128)(2,1)} %reshape.145) | data formatting | bytes 1048576 | tf_op jit(solution)/shard_map/reshape | solution.py:71
  204.9 37.0 %all_to_all.69 = bf16[128,2,64,16]{0,3,1,2:T(8,128)(2,1)S(1)} all-to-all(bf16[128,2,64,16]{0,3,1,2:T(8,128)(2,1)S(1)} %copy.94), channel_id=1, replica_groups=mesh['tok'=32,'batch'=16] {'tok'}, dimensions={2} | all-to-all | bytes 1048576 | tf_op jit(solution)/shard_map/all_to_all | solution.py:72
  242.9 3.7 %fusion.30 = f32[2,128,768]{2,1,0:T(8,128)} fusion(bf16[2,1024,768]{2,1,0:T(8,128)(2,1)} %all-gather.4.cloned.1.call-done, f32[128,2,1024]{0,2,1:T(8,128)S(1)} %bitcast.79, f32[2,1024]{1,0:T(2,128)S(1)} %copy-done.4, f32[128,2]{0,1:T(2,128)S(1)} %add_rsqrt_fusion.1), kind=kOutput, calls=%fused_computation.50 | convolution fusion | flops 403439616 | bytes 4989952 | tf_op jit(solution)/shard_map/uhd,hdf->huf/dot_general | solution.py:79
  246.6 4.5 %fusion.18 = bf16[128,2,1024]{2,0,1:T(8,128)(2,1)S(1)} fusion(f32[128,2,1024]{2,0,1:T(8,128)S(1)} %copy.100, bf16[2,768,1024]{2,1,0:T(8,128)(2,1)} %all-gather.8.cloned.1.call-done, bf16[2,1024,768]{2,1,0:T(8,128)(2,1)} %all-gather.6.cloned.1.call-done, f32[2,128,768]{2,1,0:T(8,128)} %fusion.30, f32[128,2,1024]{0,2,1:T(8,128)S(1)} %bitcast.80, ...), kind=kOutput, calls=%fused_computation.33 | convolution fusion | flops 807796736 | bytes 9708544 | tf_op jit(solution)/shard_map/huf,hfd->uhd/dot_general | solution.py:84
  251.4 37.0 %all_to_all.70 = bf16[128,2,64,16]{0,3,1,2:T(8,128)(2,1)S(1)} all-to-all(bf16[128,2,64,16]{0,3,1,2:T(8,128)(2,1)S(1)} %copy.102), channel_id=1, replica_groups=mesh['tok'=32,'batch'=16] {'tok'}, dimensions={2} | all-to-all | bytes 1048576 | tf_op jit(solution)/shard_map/all_to_all | solution.py:92
  288.4 1.1 copy.104
  (85 shorter events, 20.5 us)
Async XLA Ops:
  6.5 124.6 %copy-start = (bf16[256,1024]{1,0:T(8,128)(2,1)S(1)}, bf16[256,1024]{1,0:T(8,128)(2,1)}, u32[]{:S(2)}) copy-start(bf16[256,1024]{1,0:T(8,128)(2,1)} %param.16) | copy-start | bytes 1572868
  6.5 236.3 %all-gather.4.cloned.1.call-start = ((), (), s32[]{:S(2)}) async-start(), calls=%async_computation.7 | async-start | bytes 3342336 | tf_op jit(solution)/shard_map/all_gather | solution.py:81
  7.3 239.3 %all-gather.6.cloned.1.call-start = ((), (), s32[]{:S(2)}) async-start(), calls=%async_computation.8 | async-start | bytes 3342336 | tf_op jit(solution)/shard_map/all_gather | solution.py:82
  13.8 9.9 %copy-start.1 = (s32[4,128,1]{1,2,0:T(1,128)S(1)}, s32[4,128,1]{1,2,0:T(1,128)}, u32[]{:S(2)}) copy-start(s32[4,128,1]{1,2,0:T(1,128)} %param.13) | copy-start | bytes 6148
  17.5 51.4 %copy-start.2 = (bf16[1024,256]{1,0:T(8,128)(2,1)S(1)}, bf16[1024,256]{1,0:T(8,128)(2,1)}, u32[]{:S(2)}) copy-start(bf16[1024,256]{1,0:T(8,128)(2,1)} %param.12) | copy-start | bytes 1572868
  73.3 45.4 %copy-start.3 = (bf16[64,1024]{1,0:T(8,128)(2,1)S(1)}, bf16[64,1024]{1,0:T(8,128)(2,1)}, u32[]{:S(2)}) copy-start(bf16[64,1024]{1,0:T(8,128)(2,1)} %param.17) | copy-start | bytes 393220
  114.3 14.1 %all-to-all-start.3 = ((bf16[32,16,2,256]{3,2,0,1:T(2,128)(2,1)}), bf16[32,16,2,256]{3,2,0,1:T(2,128)(2,1)S(1)}, u32[]{:S(2)}, u32[]{:S(2)}) async-start(bf16[32,16,2,256]{3,2,0,1:T(2,128)(2,1)} %copy.87), calls=%async_computation.3 | async-start | bytes 1048576 | tf_op jit(solution)/shard_map/all_to_all | solution.py:43
  117.9 128.7 %all-gather.8.cloned.1.call-start = ((), (), s32[]{:S(2)}) async-start(), calls=%async_computation.9 | async-start | bytes 3342336 | tf_op jit(solution)/shard_map/all_gather | solution.py:87
  132.5 0.7 copy-start.5
  242.2 0.7 copy-start.4
Sparse Core Ops, SparseCore 0:
  10.4 68.4 all-gather.3
  81.9 63.3 all-gather.5
  148.3 62.2 all-gather.7
where the time goes:
time: 297 us; the launch traced here: 296 us
  blocking collectives  193 us (65%)
  local copies, waits for them, and re-layouts  45.6 us (15%)
  other arithmetic  14.5 us (5%)
  matrix products  14.4 us (5%)
  between operations  13.5 us (5%)
  waiting for transfers between devices  11.5 us (4%)
  starting transfers between devices  3.84 us (1%)
    all_to_all x1, blocking collectives, shards(): lax.all_to_all(served, 'tok', split_axis=0, concat_axis=0, tiled=True)  38.7 us
    all_to_all x1, blocking collectives, shards(): lax.all_to_all(pooled, 'tok', split_axis=1, concat_axis=0, tiled=True)  38.1 us
    all_to_all x1, blocking collectives, shards(): lax.all_to_all(spread, 'tok', split_axis=2, concat_axis=1, tiled=True)  37 us
    all_to_all x1, blocking collectives, shards(): lax.all_to_all(split_heads, 'tok', split_axis=2, concat_axis=1, tiled=True)  37 us
    all_to_all x1, blocking collectives, shards(): lax.all_to_all(request, 'tok', split_axis=0, concat_axis=0, tiled=True)  28.7 us
    all_to_all x1, blocking collectives, shards(): lax.all_to_all(lax.all_to_all(request, 'tok', split_axis=0, concat_axis=0...  13 us
    reshape x2, local copies, waits for them, and re-layouts, shards(): split_heads = regrouped.reshape(group, nquery // ntok, nquery, headsz)  9.63 us
    all_to_all x1, waiting for transfers between devices, shards(): lax.all_to_all(lax.all_to_all(served, 'tok', split_axis=0, concat_axis=0,...  9.57 us
  transfers between devices with their start and end apart: 4, of which 1 were waited for; matrix products, arithmetic and copies ran while one was open for 23% of the time, Pallas kernels for 0%

commit v1 on v0

v1 whole, which is shorter than its diff:
```python
import jax
import jax.numpy as jnp
from jax import lax
from jax.experimental import pallas as pl
from jax.experimental.pallas import tpu as pltpu
from jax.sharding import PartitionSpec as P

HEADS_STEP = 8
MASKED = -1e30
EPS = 1e-06
VMEM_BYTES = 50 * 1024 * 1024


def dot32(left, right):
    return jnp.dot(left, right, preferred_element_type=jnp.float32)


def one_hot(index, width):
    lanes = lax.broadcasted_iota(jnp.int32, (index.shape[0], width), 1)
    return jnp.where(lanes == index, 1.0, 0.0).astype(jnp.bfloat16)


def pool_kernel(len_ref, answer_ref, position_ref, w_in_ref, query_ref, out_ref, keys_ref):
    users = len_ref.shape[0]
    slots = position_ref.shape[0] // users
    steps = keys_ref.shape[0]
    step_width = keys_ref.shape[2]
    headsz = step_width // HEADS_STEP
    nquery = query_ref.shape[2]
    step = pl.program_id(0)

    @pl.when(step == 0)
    def _():
        for user in range(users):
            span = slice(user * slots, (user + 1) * slots)
            pick = one_hot(position_ref[span, :], answer_ref.shape[0])
            rows = dot32(pick, answer_ref[...]).astype(jnp.bfloat16)
            proj = dot32(rows, w_in_ref[...])
            scale = lax.rsqrt(jnp.mean(proj * proj, axis=-1, keepdims=True) + EPS)
            keys = (proj * scale).astype(jnp.bfloat16)
            for part in range(steps):
                keys_ref[part, span, :] = keys[:, part * step_width : (part + 1) * step_width]

    query = query_ref[0].astype(jnp.float32)
    wide = jnp.concatenate([query] * HEADS_STEP, axis=1)
    row_head = lax.broadcasted_iota(jnp.int32, wide.shape, 0) // headsz
    col_head = lax.broadcasted_iota(jnp.int32, wide.shape, 1) // nquery
    spread = jnp.where(row_head == col_head, wide, 0.0).astype(jnp.bfloat16)
    half_heads = HEADS_STEP // 2
    blocks = {}
    for user in range(users):
        keys = keys_ref[step, user * slots : (user + 1) * slots, :]
        scores = dot32(keys, spread)
        slot = lax.broadcasted_iota(jnp.int32, scores.shape, 0)
        scores = jnp.where(slot < len_ref[user], scores, MASKED)
        top = jnp.max(scores, axis=0, keepdims=True)
        weight = jnp.exp((scores - top) * (1.0 / headsz**0.5))
        total = jnp.sum(weight, axis=0, keepdims=True)
        attn = (weight * (1.0 / total)).astype(jnp.bfloat16)
        keys_t = keys.astype(jnp.float32).T.astype(jnp.bfloat16)
        for half in range(2):
            rows = keys_t[half * half_heads * headsz : (half + 1) * half_heads * headsz, :]
            cols = attn[:, half * half_heads * nquery : (half + 1) * half_heads * nquery]
            pooled = dot32(rows, cols)
            for head in range(half_heads):
                block = pooled[
                    head * headsz : (head + 1) * headsz, head * nquery : (head + 1) * nquery
                ]
                low = block[: headsz // 2, :]
                high = block[headsz // 2 :, :]
                blocks[user, half * half_heads + head] = jnp.concatenate([low, high], axis=1)
    for pair in range(HEADS_STEP // 2):
        stack = jnp.stack(
            [blocks[user, 2 * pair + which] for user in range(users) for which in range(2)], axis=0
        )
        turned = jnp.swapaxes(stack, 0, 1)
        row = jnp.concatenate([turned[part] for part in range(turned.shape[0])], axis=1)
        out_ref[pair, :, :] = row.astype(jnp.bfloat16)


def pool(lengths, answers, position, w_in, queries):
    users = lengths.shape[0]
    width = w_in.shape[1]
    nquery = queries.shape[0]
    headsz = width // nquery
    steps = nquery // HEADS_STEP
    step_width = width // steps
    query_t = queries.T.reshape(steps, step_width, nquery)
    pairs = nquery // 2
    return pl.pallas_call(
        pool_kernel,
        grid=(steps,),
        in_specs=[
            pl.BlockSpec(memory_space=pltpu.SMEM),
            pl.BlockSpec(answers.shape, lambda i: (0, 0)),
            pl.BlockSpec(position.shape, lambda i: (0, 0)),
            pl.BlockSpec(w_in.shape, lambda i: (0, 0)),
            pl.BlockSpec((1, step_width, nquery), lambda i: (i, 0, 0)),
        ],
        out_specs=pl.BlockSpec((HEADS_STEP // 2, 2 * users, width), lambda i: (i, 0, 0)),
        out_shape=jax.ShapeDtypeStruct((pairs, 2 * users, width), jnp.bfloat16),
        scratch_shapes=[pltpu.VMEM((steps, position.shape[0], step_width), jnp.bfloat16)],
        compiler_params=pltpu.CompilerParams(vmem_limit_bytes=VMEM_BYTES),
    )(lengths, answers, position, w_in, query_t)


def net_kernel(mixed_ref, gain_ref, weight_ref, out_ref, gate_ref, up_ref, down_ref, sems):
    tokens = gain_ref.shape[0]
    rows, width = mixed_ref.shape
    group = rows // tokens
    nparts, _, part_rows, hidden_width = weight_ref.shape
    down_rows = down_ref.shape[2]
    rest = width - hidden_width
    headsz = out_ref.shape[3]
    copies = []
    for token in range(tokens):
        pieces = [
            (weight_ref.at[:, token, :, :], gate_ref.at[token]),
            (weight_ref.at[:, tokens + token, :, :], up_ref.at[token]),
            (
                weight_ref.at[:, 2 * tokens + token, pl.ds(0, down_rows), :],
                down_ref.at[token, :, :, pl.ds(0, hidden_width)],
            ),
        ]
        extra = part_rows - down_rows
        for piece in range(down_rows // extra):
            pieces.append(
                (
                    weight_ref.at[
                        :, 2 * tokens + token, pl.ds(down_rows, extra), pl.ds(piece * rest, rest)
                    ],
                    down_ref.at[token, :, pl.ds(piece * extra, extra), pl.ds(hidden_width, rest)],
                )
            )
        copies.append(
            [
                pltpu.make_async_copy(src, dst, sems.at[token, number])
                for number, (src, dst) in enumerate(pieces)
            ]
        )
    for some in copies:
        for copy in some:
            copy.start()
    target = lax.broadcasted_iota(jnp.int32, (rows, 1), 0)
    order = (target % group) * tokens + target // group
    sorted_rows = dot32(one_hot(order, rows), mixed_ref[...]).astype(jnp.bfloat16)
    nquery = width // headsz
    spot = lax.broadcasted_iota(jnp.int32, (width, 1), 0)
    feature = spot % nquery * headsz + (spot // nquery % 2) * (headsz // 2) + spot // (2 * nquery)
    mixed = dot32(sorted_rows, one_hot(feature, width))
    for token in range(tokens):
        wide = mixed[token * group : (token + 1) * group, :]
        scale = lax.rsqrt(jnp.mean(wide * wide, axis=-1, keepdims=True) + EPS)
        normed = (wide * scale * gain_ref[token : token + 1, :]).astype(jnp.bfloat16)
        copies[token][0].wait()
        gate = dot32(normed, gate_ref[token].reshape(width, hidden_width))
        copies[token][1].wait()
        up_val = dot32(normed, up_ref[token].reshape(width, hidden_width))
        hidden = (gate / (1.0 + jnp.exp(-gate)) * up_val).astype(jnp.bfloat16)
        for copy in copies[token][2:]:
            copy.wait()
        down = dot32(hidden, down_ref[token].reshape(hidden_width, width))
        summed = (wide + down).T.astype(jnp.bfloat16)
        out_ref[:, :, token, :, :] = summed.reshape(
            out_ref.shape[0], out_ref.shape[1], headsz, group
        )


def net(mixed, gain, weights, ntok):
    rows, width = mixed.shape
    tokens = gain.shape[0]
    group = rows // tokens
    nparts, _, part_rows, hidden_width = weights.shape
    down_rows = hidden_width // nparts
    nquery = ntok * tokens
    pieces = 3 + down_rows // (part_rows - down_rows)
    return pl.pallas_call(
        net_kernel,
        in_specs=[
            pl.BlockSpec(memory_space=pltpu.VMEM),
            pl.BlockSpec(memory_space=pltpu.VMEM),
            pl.BlockSpec(memory_space=pl.ANY),
        ],
        out_specs=pl.BlockSpec(memory_space=pltpu.VMEM),
        out_shape=jax.ShapeDtypeStruct(
            (ntok, tokens, tokens, width // nquery, group), jnp.bfloat16
        ),
        scratch_shapes=[
            pltpu.VMEM((tokens, nparts, part_rows, hidden_width), jnp.bfloat16),
            pltpu.VMEM((tokens, nparts, part_rows, hidden_width), jnp.bfloat16),
            pltpu.VMEM((tokens, nparts, down_rows, width), jnp.bfloat16),
            pltpu.SemaphoreType.DMA((tokens, pieces)),
        ],
        compiler_params=pltpu.CompilerParams(vmem_limit_bytes=VMEM_BYTES),
    )(mixed, gain, weights)


def pack_weights(w_gate, w_up, w_down):
    hidden_width = w_gate.shape[2]
    rest = w_down.shape[2] - hidden_width
    extra = w_gate.shape[1] - w_down.shape[1]
    pieces = [
        w_down[:, at : at + extra, hidden_width:] for at in range(0, w_down.shape[1], extra)
    ]
    tail = jnp.concatenate(pieces, axis=2)
    down = jnp.concatenate([w_down[:, :, :hidden_width], tail], axis=1)
    return jnp.concatenate([w_gate, w_up, down], axis=0)


def shards(table, hist_owner, hist_row, hist_len, w_in, queries, ffn_gain, w_gate, w_up, w_down):
    ntok = lax.axis_size("tok")
    nbatch = lax.axis_size("batch")
    devices = ntok * nbatch
    users, slots = hist_row.shape
    emb = table.shape[1]
    width = w_in.shape[1]
    nquery = queries.shape[0]
    headsz = width // nquery
    count = users * slots
    cap = 2 * count // devices
    weights = lax.all_gather(pack_weights(w_gate, w_up, w_down)[None], "batch", axis=0, tiled=True)

    owners = hist_owner.reshape(count)
    places = jnp.arange(count, dtype=jnp.int32)
    same = (owners[:, None] == owners[None, :]) & (places[None, :] < places[:, None])
    rank = jnp.sum(same.astype(jnp.int32), axis=1)
    position = owners * cap + rank
    spots = jnp.arange(devices * cap, dtype=jnp.int32)
    request = jnp.sum(
        jnp.where(position[:, None] == spots[None, :], hist_row.reshape(count)[:, None], 0), axis=0
    )
    asked = lax.all_to_all(request.reshape(ntok, nbatch * cap), "tok", 0, 0, tiled=True)
    asked = asked.reshape(ntok, nbatch, cap).transpose(1, 0, 2).reshape(nbatch, ntok * cap)
    asked = lax.all_to_all(asked, "batch", 0, 0, tiled=True)
    wanted = asked.reshape(nbatch, ntok, cap).transpose(1, 0, 2).reshape(devices * cap)
    local = jnp.arange(table.shape[0], dtype=jnp.int32)
    served = jnp.dot(
        (wanted[:, None] == local[None, :]).astype(jnp.bfloat16),
        table,
        preferred_element_type=jnp.bfloat16,
    )
    answers = lax.all_to_all(
        served.reshape(devices, cap, emb), ("tok", "batch"), 0, 0, tiled=True
    ).reshape(devices * cap, emb)
    pooled = pool(hist_len, answers, position.reshape(count, 1), w_in, queries)
    mixed = lax.all_to_all(pooled, "tok", 0, 0, tiled=True)
    group = users * ntok
    tokens = nquery // ntok
    sent = net(mixed.reshape(group * tokens, width), ffn_gain, weights, ntok)
    back = lax.all_to_all(sent, "tok", 0, 0, tiled=True)
    return back.transpose(4, 1, 0, 2, 3).reshape(group, tokens, width)


def solution(mesh):
    placed = (
        P(("tok", "batch"), None),
        P(("batch", "tok"), None, None),
        P(("batch", "tok"), None),
        P(("batch", "tok")),
        P(),
        P(),
        P("tok", None),
        P("tok", "batch", None),
        P("tok", "batch", None),
        P("tok", "batch", None),
    )
    return jax.shard_map(
        shards, mesh=mesh, in_specs=placed, out_specs=P("batch", "tok", None), check_vma=False
    )
```

time: 297 us -> 201 us (0.68)
  blocking collectives: 193 us -> 115 us
  local copies, waits for them, and re-layouts: 45.6 us -> 5.23 us
  waiting for transfers between devices: 11.5 us -> 35.7 us
  Pallas kernels: 0 us -> 16.9 us
  matrix products: 14.4 us -> 0.84 us
  other arithmetic: 14.5 us -> 2.45 us
  starting transfers between devices: 3.84 us -> 10.7 us
    all_to_all x6 -> x4, blocking collectives: 193 us -> 115 us  [the longest x1 37 us: shards(): back = lax.all_to_all(sent, 'tok', 0, 0, tiled=True)]
    all_to_all x1, waiting for transfers between devices: 9.57 us -> 35.7 us  [shards(): lax.all_to_all(served.reshape(devices, cap, emb), ('tok', 'batch'), 0, 0,...]
    pallas_call x0 -> x2, Pallas kernels: none -> 16.9 us  [the longest x1 12.5 us: pool(): pl.pallas_call(pool_kernel, grid=(steps,), in_specs=[pl.BlockSpec(memory_...]
    dot_general x11 -> x1, matrix products: 14.4 us -> 0.84 us  [shards(): jnp.dot((wanted[:, None] == local[None, :]).astype(jnp.bfloat16), table,...]
    gather x5 -> x0, local copies, waits for them, and re-layouts: 13.3 us -> none  [the longest x2 4.14 us: shards(): jnp.take(table, received.reshape(-1), axis=0)]
    reshape x9 -> x3, local copies, waits for them, and re-layouts: 11.9 us -> 2.31 us  [the longest x1 1.12 us: shards(): return back.transpose(4, 1, 0, 2, 3).reshape(group, tokens, width)]
    dynamic_update_slice x8 -> x0, local copies, waits for them, and re-layouts: 8.01 us -> none  [shards(): pooled = lax.map(attend, (keys, hist_len))]
    all_to_all x1, starting transfers between devices: 3.57 us -> 10.7 us  [shards(): lax.all_to_all(served.reshape(devices, cap, emb), ('tok', 'batch'), 0, 0,...]
  transfers between devices with their start and end apart: 4 -> 2, of which waited for: 1 -> 1; matrix products, arithmetic and copies ran while one was open for 23% -> 2% of each run, Pallas kernels for 0% -> 6%
where the time goes in v1:
time: 201 us
  blocking collectives  115 us (57%)
  waiting for transfers between devices  35.7 us (18%)
  Pallas kernels  16.9 us (8%)
  between operations  13.5 us (7%)
  starting transfers between devices  10.7 us (5%)
  local copies, waits for them, and re-layouts  5.23 us (3%)
  other arithmetic  2.45 us (1%)
    all_to_all x1, blocking collectives, shards(): back = lax.all_to_all(sent, 'tok', 0, 0, tiled=True)  37 us
    all_to_all x1, blocking collectives, shards(): mixed = lax.all_to_all(pooled, 'tok', 0, 0, tiled=True)  36.9 us
    all_to_all x1, waiting for transfers between devices, shards(): lax.all_to_all(served.reshape(devices, cap, emb), ('tok', 'batch'), 0, 0,...  35.7 us
    all_to_all x1, blocking collectives, shards(): lax.all_to_all(request.reshape(ntok, nbatch * cap), 'tok', 0, 0, tiled=True)  28.3 us
    all_to_all x1, blocking collectives, shards(): asked = lax.all_to_all(asked, 'batch', 0, 0, tiled=True)  13 us
    pallas_call x1, Pallas kernels, pool(): pl.pallas_call(pool_kernel, grid=(steps,), in_specs=[pl.BlockSpec(memory_...  12.5 us
    all_to_all x1, starting transfers between devices, shards(): lax.all_to_all(served.reshape(devices, cap, emb), ('tok', 'batch'), 0, 0,...  10.7 us
    pallas_call x1, Pallas kernels, net(): pl.pallas_call(net_kernel, in_specs=[pl.BlockSpec(memory_space=pltpu.VMEM...  4.3 us
  transfers between devices with their start and end apart: 2, of which 1 were waited for; matrix products, arithmetic and copies ran while one was open for 2% of the time, Pallas kernels for 6%

profile of v1, /device:TPU:1, one launch (start us, length us, event | category | flops | bytes accessed | tf_op | source)
XLA Modules:
  0.0 200.6 jit_solution(13380978982648863901)
XLA Ops:
  6.5 0.0 copy-start
  6.5 0.8 fusion.3
  7.4 0.9 slice.12
  8.3 1.9 maximum_maximum_fusion
  10.2 0.0 all-gather.3.cloned.1.call-update
  10.2 0.2 convert_reduce_fusion
  10.5 0.3 select_reduce_fusion
  10.8 0.1 all_to_all.21
  10.9 28.3 %all_to_all.33 = s32[32,1,32]{2,1,0:T(1,128)S(1)} all-to-all(s32[32,1,32]{2,1,0:T(1,128)S(1)} %bitcast.29), channel_id=1, replica_groups=mesh['tok'=32,'batch'=16] {'tok'}, dimensions={0} | all-to-all | bytes 8192 | tf_op jit(solution)/shard_map/all_to_all | solution.py:232
  39.2 0.1 copy.50
  39.3 0.1 copy.51
  39.3 0.1 copy.52
  39.4 13.0 %all_to_all.34 = s32[16,1,64]{2,1,0:T(1,128)S(1)} all-to-all(s32[16,1,64]{2,1,0:T(1,128)S(1)} %copy.52), channel_id=1, replica_groups=mesh['tok'=32,'batch'=16] {'batch'}, dimensions={0} | all-to-all | bytes 8192 | tf_op jit(solution)/shard_map/all_to_all | solution.py:234
  52.4 0.1 copy.53
  52.5 0.3 copy.54
  52.7 0.2 eq.47
  52.9 0.8 fusion
  53.7 0.0 copy-start.4
  53.8 1.0 reshape.62
  54.8 10.7 %all-to-all-start.2 = ((bf16[512,2,256]{2,1,0:T(2,128)(2,1)}), bf16[512,2,256]{2,1,0:T(2,128)(2,1)S(1)}, u32[]{:S(2)}, u32[]{:S(2)}) async-start(bf16[512,2,256]{2,1,0:T(2,128)(2,1)} %reshape.62), calls=%async_computation.2 | async-start | bytes 1048576 | tf_op jit(solution)/shard_map/all_to_all | solution.py:242
  65.5 0.1 copy.56.position_ref
  65.6 0.2 copy.55
  65.8 35.7 %all-to-all-done.2 = bf16[512,2,256]{2,1,0:T(2,128)(2,1)S(1)} async-done(((bf16[512,2,256]{2,1,0:T(2,128)(2,1)}), bf16[512,2,256]{2,1,0:T(2,128)(2,1)S(1)}, u32[]{:S(2)}, u32[]{:S(2)}) %all-to-all-start.2) | async-done | bytes 524320 | tf_op jit(solution)/shard_map/all_to_all | solution.py:242
  101.5 0.2 reshape.63.answer_ref
  101.7 0.0 copy-done.1
  101.7 0.0 copy-done.3
  101.8 0.0 copy-start.2
  101.8 12.5 %shard_map.100 = bf16[32,8,1024]{2,1,0:T(8,128)(2,1)S(1)} custom-call(s32[4]{0:T(128)S(1)} %copy-done.3, bf16[1024,256]{1,0:T(8,128)(2,1)S(1)} %reshape.63.answer_ref, s32[512,1]{1,0:T(8,128)S(1)} %copy.56.position_ref, bf16[256,1024]{1,0:T(8,128)(2,1)S(1)} %copy-done.1, bf16[8,128,64]{2,1,0:T(8,128)(2,1)S(1)} %bitcast.21), custom_call_target="tpu_custom_call" | custom-call | tf_op jit(solution)/shard_map/pallas_call | solution.py:90
  114.3 36.9 %all_to_all.35 = bf16[32,8,1024]{2,1,0:T(8,128)(2,1)S(1)} all-to-all(bf16[32,8,1024]{2,1,0:T(8,128)(2,1)S(1)} %shard_map.100), channel_id=1, replica_groups=mesh['tok'=32,'batch'=16] {'tok'}, dimensions={0} | all-to-all | bytes 1048576 | tf_op jit(solution)/shard_map/all_to_all | solution.py:246
  151.3 4.3 %shard_map.101 = bf16[32,2,2,16,128]{4,3,2,1,0:T(8,128)(2,1)S(1)} custom-call(bf16[256,1024]{1,0:T(8,128)(2,1)S(1)} %bitcast.20, f32[2,1024]{1,0:T(2,128)S(1)} %copy-done.2, bf16[16,6,64,768]{3,2,1,0:T(8,128)(2,1)} %bitcast.22), custom_call_target="tpu_custom_call" | custom-call | tf_op jit(solution)/shard_map/pallas_call | solution.py:177
  155.6 37.0 %all_to_all.36 = bf16[32,2,2,16,128]{4,3,2,1,0:T(8,128)(2,1)S(1)} all-to-all(bf16[32,2,2,16,128]{4,3,2,1,0:T(8,128)(2,1)S(1)} %shard_map.101), channel_id=1, replica_groups=mesh['tok'=32,'batch'=16] {'tok'}, dimensions={0} | all-to-all | bytes 1048576 | tf_op jit(solution)/shard_map/all_to_all | solution.py:250
  192.6 1.1 copy.58
  (14 shorter events, 0.1 us)
Async XLA Ops:
  6.5 46.4 %copy-start = (bf16[1024,256]{1,0:T(8,128)(2,1)S(1)}, bf16[1024,256]{1,0:T(8,128)(2,1)}, u32[]{:S(2)}) copy-start(bf16[1024,256]{1,0:T(8,128)(2,1)} %param.10) | copy-start | bytes 1572868
  6.5 3.7 %copy-start.5 = (s32[4,128,1]{1,2,0:T(1,128)S(1)}, s32[4,128,1]{1,2,0:T(1,128)}, u32[]{:S(2)}) copy-start(s32[4,128,1]{1,2,0:T(1,128)} %param.11) | copy-start | bytes 6148
  6.5 3.9 %copy-start.6 = (s32[4,128]{1,0:T(4,128)S(1)}, s32[4,128]{1,0:T(4,128)}, u32[]{:S(2)}) copy-start(s32[4,128]{1,0:T(4,128)} %param.12) | copy-start | bytes 6148
  6.5 144.7 %all-gather.3.cloned.1.call-start = ((), (), s32[]{:S(2)}) async-start(), calls=%async_computation.5 | async-start | bytes 10027008 | tf_op jit(solution)/shard_map/all_gather | solution.py:221
  53.7 11.9 %copy-start.4 = (bf16[64,1024]{1,0:T(8,128)(2,1)S(1)}, bf16[64,1024]{1,0:T(8,128)(2,1)}, u32[]{:S(2)}) copy-start(bf16[64,1024]{1,0:T(8,128)(2,1)} %param.15) | copy-start | bytes 393220
  54.7 47.0 %copy-start.1 = (bf16[256,1024]{1,0:T(8,128)(2,1)S(1)}, bf16[256,1024]{1,0:T(8,128)(2,1)}, u32[]{:S(2)}) copy-start(bf16[256,1024]{1,0:T(8,128)(2,1)} %w_in_ref.1) | copy-start | bytes 1572868
  54.7 47.0 %copy-start.3 = (s32[4]{0:T(128)S(1)}, s32[4]{0:T(128)}, u32[]{:S(2)}) copy-start(s32[4]{0:T(128)} %len_ref.1) | copy-start | bytes 52
  54.8 46.8 %all-to-all-start.2 = ((bf16[512,2,256]{2,1,0:T(2,128)(2,1)}), bf16[512,2,256]{2,1,0:T(2,128)(2,1)S(1)}, u32[]{:S(2)}, u32[]{:S(2)}) async-start(bf16[512,2,256]{2,1,0:T(2,128)(2,1)} %reshape.62), calls=%async_computation.2 | async-start | bytes 1048576 | tf_op jit(solution)/shard_map/all_to_all | solution.py:242
  101.8 49.5 %copy-start.2 = (f32[2,1024]{1,0:T(2,128)S(1)}, f32[2,1024]{1,0:T(2,128)}, u32[]{:S(2)}) copy-start(f32[2,1024]{1,0:T(2,128)} %gain_ref.1) | copy-start | bytes 24580
Sparse Core Ops, SparseCore 0:
  10.4 101.9 all-gather.2

commit v2 on v1

--- a/solution.py
+++ b/solution.py
@@ -6,7 +6,9 @@
 from jax.sharding import PartitionSpec as P
 
 HEADS_STEP = 8
+INNER = 4
 MASKED = -1e30
+LOG2E = 1.4426950408889634
 EPS = 1e-06
 VMEM_BYTES = 50 * 1024 * 1024
 
@@ -23,10 +25,9 @@
 def pool_kernel(len_ref, answer_ref, position_ref, w_in_ref, query_ref, out_ref, keys_ref):
     users = len_ref.shape[0]
     slots = position_ref.shape[0] // users
-    steps = keys_ref.shape[0]
-    step_width = keys_ref.shape[2]
+    inner, step_width, nquery = query_ref.shape
     headsz = step_width // HEADS_STEP
-    nquery = query_ref.shape[2]
+    heads = HEADS_STEP // 2
     step = pl.program_id(0)
 
     @pl.when(step == 0)
@@ -38,68 +39,66 @@
             proj = dot32(rows, w_in_ref[...])
             scale = lax.rsqrt(jnp.mean(proj * proj, axis=-1, keepdims=True) + EPS)
             keys = (proj * scale).astype(jnp.bfloat16)
-            for part in range(steps):
+            for part in range(keys_ref.shape[0]):
                 keys_ref[part, span, :] = keys[:, part * step_width : (part + 1) * step_width]
 
-    query = query_ref[0].astype(jnp.float32)
-    wide = jnp.concatenate([query] * HEADS_STEP, axis=1)
-    row_head = lax.broadcasted_iota(jnp.int32, wide.shape, 0) // headsz
-    col_head = lax.broadcasted_iota(jnp.int32, wide.shape, 1) // nquery
-    spread = jnp.where(row_head == col_head, wide, 0.0).astype(jnp.bfloat16)
-    half_heads = HEADS_STEP // 2
-    blocks = {}
-    for user in range(users):
-        keys = keys_ref[step, user * slots : (user + 1) * slots, :]
-        scores = dot32(keys, spread)
-        slot = lax.broadcasted_iota(jnp.int32, scores.shape, 0)
-        scores = jnp.where(slot < len_ref[user], scores, MASKED)
-        top = jnp.max(scores, axis=0, keepdims=True)
-        weight = jnp.exp((scores - top) * (1.0 / headsz**0.5))
-        total = jnp.sum(weight, axis=0, keepdims=True)
-        attn = (weight * (1.0 / total)).astype(jnp.bfloat16)
-        keys_t = keys.astype(jnp.float32).T.astype(jnp.bfloat16)
+    for sub in range(inner):
+        query = query_ref[sub].astype(jnp.float32)
+        wide = jnp.concatenate([query] * heads, axis=1)
+        row_head = lax.broadcasted_iota(jnp.int32, wide.shape, 0) // headsz
+        col_head = lax.broadcasted_iota(jnp.int32, wide.shape, 1) // nquery
+        blocks = {}
         for half in range(2):
-            rows = keys_t[half * half_heads * headsz : (half + 1) * half_heads * headsz, :]
-            cols = attn[:, half * half_heads * nquery : (half + 1) * half_heads * nquery]
-            pooled = dot32(rows, cols)
-            for head in range(half_heads):
-                block = pooled[
-                    head * headsz : (head + 1) * headsz, head * nquery : (head + 1) * nquery
-                ]
-                low = block[: headsz // 2, :]
-                high = block[headsz // 2 :, :]
-                blocks[user, half * half_heads + head] = jnp.concatenate([low, high], axis=1)
-    for pair in range(HEADS_STEP // 2):
-        stack = jnp.stack(
-            [blocks[user, 2 * pair + which] for user in range(users) for which in range(2)], axis=0
-        )
-        turned = jnp.swapaxes(stack, 0, 1)
-        row = jnp.concatenate([turned[part] for part in range(turned.shape[0])], axis=1)
-        out_ref[pair, :, :] = row.astype(jnp.bfloat16)
+            spread = jnp.where(row_head == col_head + half * heads, wide, 0.0).astype(jnp.bfloat16)
+            for user in range(users):
+                keys = keys_ref[step * inner + sub, user * slots : (user + 1) * slots, :]
+                scores = dot32(keys, spread)
+                slot = lax.broadcasted_iota(jnp.int32, scores.shape, 0)
+                scores = jnp.where(slot < len_ref[user], scores, MASKED)
+                top = jnp.max(scores, axis=0, keepdims=True)
+                weight = jnp.exp2((scores - top) * (LOG2E / headsz**0.5))
+                total = jnp.sum(weight, axis=0, keepdims=True)
+                attn = (weight * (1.0 / total)).astype(jnp.bfloat16)
+                pooled = lax.dot_general(
+                    keys, attn, (((0,), (0,)), ((), ())), preferred_element_type=jnp.float32
+                )
+                for head in range(heads):
+                    at = (half * heads + head) * headsz
+                    block = pooled[at : at + headsz, head * nquery : (head + 1) * nquery]
+                    low = block[: headsz // 2, :]
+                    high = block[headsz // 2 :, :]
+                    blocks[user, half * heads + head] = jnp.concatenate([low, high], axis=1)
+        for pair in range(heads):
+            stack = jnp.stack(
+                [blocks[user, 2 * pair + which] for user in range(users) for which in range(2)],
+                axis=0,
+            )
+            turned = jnp.swapaxes(stack, 0, 1)
+            row = jnp.concatenate([turned[part] for part in range(turned.shape[0])], axis=1)
+            out_ref[sub * heads + pair, :, :] = row.astype(jnp.bfloat16)
 
 
 def pool(lengths, answers, position, w_in, queries):
     users = lengths.shape[0]
     width = w_in.shape[1]
     nquery = queries.shape[0]
-    headsz = width // nquery
-    steps = nquery // HEADS_STEP
-    step_width = width // steps
-    query_t = queries.T.reshape(steps, step_width, nquery)
+    parts = nquery // HEADS_STEP
+    step_width = width // parts
+    query_t = queries.T.reshape(parts, step_width, nquery)
     pairs = nquery // 2
     return pl.pallas_call(
         pool_kernel,
-        grid=(steps,),
+        grid=(parts // INNER,),
         in_specs=[
             pl.BlockSpec(memory_space=pltpu.SMEM),
             pl.BlockSpec(answers.shape, lambda i: (0, 0)),
             pl.BlockSpec(position.shape, lambda i: (0, 0)),
             pl.BlockSpec(w_in.shape, lambda i: (0, 0)),
-            pl.BlockSpec((1, step_width, nquery), lambda i: (i, 0, 0)),
+            pl.BlockSpec((INNER, step_width, nquery), lambda i: (i, 0, 0)),
         ],
-        out_specs=pl.BlockSpec((HEADS_STEP // 2, 2 * users, width), lambda i: (i, 0, 0)),
+        out_specs=pl.BlockSpec((INNER * HEADS_STEP // 2, 2 * users, width), lambda i: (i, 0, 0)),
         out_shape=jax.ShapeDtypeStruct((pairs, 2 * users, width), jnp.bfloat16),
-        scratch_shapes=[pltpu.VMEM((steps, position.shape[0], step_width), jnp.bfloat16)],
+        scratch_shapes=[pltpu.VMEM((parts, position.shape[0], step_width), jnp.bfloat16)],
         compiler_params=pltpu.CompilerParams(vmem_limit_bytes=VMEM_BYTES),
     )(lengths, answers, position, w_in, query_t)
 
@@ -195,16 +194,26 @@
     )(mixed, gain, weights)
 
 
+def pack_kernel(gate_ref, up_ref, down_ref, out_ref):
+    tokens, part_rows, hidden_width = gate_ref.shape
+    _, down_rows, width = down_ref.shape
+    rest = width - hidden_width
+    extra = part_rows - down_rows
+    out_ref[:tokens] = gate_ref[...]
+    out_ref[tokens : 2 * tokens] = up_ref[...]
+    out_ref[2 * tokens :, :down_rows, :] = down_ref[:, :, :hidden_width]
+    for piece in range(down_rows // extra):
+        out_ref[2 * tokens :, down_rows:, piece * rest : (piece + 1) * rest] = down_ref[
+            :, piece * extra : (piece + 1) * extra, hidden_width:
+        ]
+
+
 def pack_weights(w_gate, w_up, w_down):
-    hidden_width = w_gate.shape[2]
-    rest = w_down.shape[2] - hidden_width
-    extra = w_gate.shape[1] - w_down.shape[1]
-    pieces = [
-        w_down[:, at : at + extra, hidden_width:] for at in range(0, w_down.shape[1], extra)
-    ]
-    tail = jnp.concatenate(pieces, axis=2)
-    down = jnp.concatenate([w_down[:, :, :hidden_width], tail], axis=1)
-    return jnp.concatenate([w_gate, w_up, down], axis=0)
+    tokens, part_rows, hidden_width = w_gate.shape
+    return pl.pallas_call(
+        pack_kernel,
+        out_shape=jax.ShapeDtypeStruct((3 * tokens, part_rows, hidden_width), jnp.bfloat16),
+    )(w_gate, w_up, w_down)
 
 
 def shards(table, hist_owner, hist_row, hist_len, w_in, queries, ffn_gain, w_gate, w_up, w_down):

time: 201 us -> 194 us (0.965)
  Pallas kernels: 16.9 us -> 12 us
    pallas_call x1 -> x2, Pallas kernels: 12.5 us -> 7.74 us  [the longest x1 5.71 us: pool(): pl.pallas_call(pool_kernel, grid=(parts // INNER,), in_specs=[pl.BlockSpe...]
  transfers between devices with their start and end apart: 2 -> 2, of which waited for: 1 -> 1; matrix products, arithmetic and copies ran while one was open for 2% -> 3% of each run, Pallas kernels for 6% -> 3%
where the time goes in v2:
time: 194 us
  blocking collectives  115 us (59%)
  waiting for transfers between devices  35.7 us (18%)
  between operations  13.5 us (7%)
  Pallas kernels  12 us (6%)
  starting transfers between devices  10.6 us (5%)
  local copies, waits for them, and re-layouts  3.5 us (2%)
  other arithmetic  2.66 us (1%)
    all_to_all x1, blocking collectives, shards(): back = lax.all_to_all(sent, 'tok', 0, 0, tiled=True)  37 us
    all_to_all x1, blocking collectives, shards(): mixed = lax.all_to_all(pooled, 'tok', 0, 0, tiled=True)  36.9 us
    all_to_all x1, waiting for transfers between devices, shards(): lax.all_to_all(served.reshape(devices, cap, emb), ('tok', 'batch'), 0, 0,...  35.7 us
    all_to_all x1, blocking collectives, shards(): lax.all_to_all(request.reshape(ntok, nbatch * cap), 'tok', 0, 0, tiled=True)  28.3 us
    all_to_all x1, blocking collectives, shards(): asked = lax.all_to_all(asked, 'batch', 0, 0, tiled=True)  13 us
    all_to_all x1, starting transfers between devices, shards(): lax.all_to_all(served.reshape(devices, cap, emb), ('tok', 'batch'), 0, 0,...  10.6 us
    pallas_call x1, Pallas kernels, pool(): pl.pallas_call(pool_kernel, grid=(parts // INNER,), in_specs=[pl.BlockSpe...  5.71 us
    pallas_call x1, Pallas kernels, net(): pl.pallas_call(net_kernel, in_specs=[pl.BlockSpec(memory_space=pltpu.VMEM...  4.31 us
  transfers between devices with their start and end apart: 2, of which 1 were waited for; matrix products, arithmetic and copies ran while one was open for 3% of the time, Pallas kernels for 3%

profile of v2, /device:TPU:1, one launch (start us, length us, event | category | flops | bytes accessed | tf_op | source)
XLA Modules:
  0.0 194.1 jit_solution(13867903418671234473)
XLA Ops:
  6.5 0.0 copy-start
  6.5 2.0 %shard_map.101 = bf16[6,64,768]{2,1,0:T(8,128)(2,1)} custom-call(bf16[2,64,768]{2,1,0:T(8,128)(2,1)} %gate_ref.1, bf16[2,64,768]{2,1,0:T(8,128)(2,1)} %up_ref.1, bf16[2,48,1024]{2,1,0:T(8,128)(2,1)} %down_ref.1), custom_call_target="tpu_custom_call" | custom-call | tf_op jit(solution)/shard_map/pallas_call | solution.py:213
  8.6 0.0 all-gather.3.cloned.1.call-update
  8.6 1.0 convert_reduce_fusion
  9.6 0.7 multiply_add_fusion
  10.3 1.0 select_reduce_fusion
  11.3 0.1 all_to_all.21
  11.3 28.3 %all_to_all.33 = s32[32,1,32]{2,1,0:T(1,128)S(1)} all-to-all(s32[32,1,32]{2,1,0:T(1,128)S(1)} %bitcast.29), channel_id=1, replica_groups=mesh['tok'=32,'batch'=16] {'tok'}, dimensions={0} | all-to-all | bytes 8192 | tf_op jit(solution)/shard_map/all_to_all | solution.py:241
  39.7 0.1 copy.50
  39.7 0.1 copy.51
  39.8 0.1 copy.52
  39.9 13.0 %all_to_all.34 = s32[16,1,64]{2,1,0:T(1,128)S(1)} all-to-all(s32[16,1,64]{2,1,0:T(1,128)S(1)} %copy.52), channel_id=1, replica_groups=mesh['tok'=32,'batch'=16] {'batch'}, dimensions={0} | all-to-all | bytes 8192 | tf_op jit(solution)/shard_map/all_to_all | solution.py:243
  52.9 0.1 copy.53
  52.9 0.3 copy.54
  53.2 0.2 eq.47
  53.4 0.0 copy-start.5
  53.4 0.0 copy-start.4
  53.4 0.8 fusion
  54.2 0.0 copy-start.1
  54.3 0.0 copy-start.3
  54.3 1.0 reshape.62
  55.3 10.6 %all-to-all-start.2 = ((bf16[512,2,256]{2,1,0:T(2,128)(2,1)}), bf16[512,2,256]{2,1,0:T(2,128)(2,1)S(1)}, u32[]{:S(2)}, u32[]{:S(2)}) async-start(bf16[512,2,256]{2,1,0:T(2,128)(2,1)} %reshape.62), calls=%async_computation.2 | async-start | bytes 1048576 | tf_op jit(solution)/shard_map/all_to_all | solution.py:251
  65.9 0.1 copy.56.position_ref
  66.0 0.2 copy.55
  66.2 0.0 copy-start.2
  66.2 35.7 %all-to-all-done.2 = bf16[512,2,256]{2,1,0:T(2,128)(2,1)S(1)} async-done(((bf16[512,2,256]{2,1,0:T(2,128)(2,1)}), bf16[512,2,256]{2,1,0:T(2,128)(2,1)S(1)}, u32[]{:S(2)}, u32[]{:S(2)}) %all-to-all-start.2) | async-done | bytes 524320 | tf_op jit(solution)/shard_map/all_to_all | solution.py:251
  101.9 0.2 reshape.63.answer_ref
  102.1 5.7 %shard_map.100 = bf16[32,8,1024]{2,1,0:T(8,128)(2,1)S(1)} custom-call(s32[4]{0:T(128)S(1)} %copy-done.3, bf16[1024,256]{1,0:T(8,128)(2,1)S(1)} %reshape.63.answer_ref, s32[512,1]{1,0:T(8,128)S(1)} %copy.56.position_ref, bf16[256,1024]{1,0:T(8,128)(2,1)S(1)} %copy-done.1, bf16[8,128,64]{2,1,0:T(8,128)(2,1)S(1)} %bitcast.21), custom_call_target="tpu_custom_call" | custom-call | tf_op jit(solution)/shard_map/pallas_call | solution.py:89
  107.8 36.9 %all_to_all.35 = bf16[32,8,1024]{2,1,0:T(8,128)(2,1)S(1)} all-to-all(bf16[32,8,1024]{2,1,0:T(8,128)(2,1)S(1)} %shard_map.100), channel_id=1, replica_groups=mesh['tok'=32,'batch'=16] {'tok'}, dimensions={0} | all-to-all | bytes 1048576 | tf_op jit(solution)/shard_map/all_to_all | solution.py:255
  144.8 4.3 %shard_map.102 = bf16[32,2,2,16,128]{4,3,2,1,0:T(8,128)(2,1)S(1)} custom-call(bf16[256,1024]{1,0:T(8,128)(2,1)S(1)} %bitcast.20, f32[2,1024]{1,0:T(2,128)S(1)} %copy-done.2, bf16[16,6,64,768]{3,2,1,0:T(8,128)(2,1)} %bitcast.22), custom_call_target="tpu_custom_call" | custom-call | tf_op jit(solution)/shard_map/pallas_call | solution.py:176
  149.1 37.0 %all_to_all.36 = bf16[32,2,2,16,128]{4,3,2,1,0:T(8,128)(2,1)S(1)} all-to-all(bf16[32,2,2,16,128]{4,3,2,1,0:T(8,128)(2,1)S(1)} %shard_map.102), channel_id=1, replica_groups=mesh['tok'=32,'batch'=16] {'tok'}, dimensions={0} | all-to-all | bytes 1048576 | tf_op jit(solution)/shard_map/all_to_all | solution.py:259
  186.1 1.1 copy.58
  (10 shorter events, 0.1 us)
Async XLA Ops:
  6.5 46.8 %copy-start = (bf16[1024,256]{1,0:T(8,128)(2,1)S(1)}, bf16[1024,256]{1,0:T(8,128)(2,1)}, u32[]{:S(2)}) copy-start(bf16[1024,256]{1,0:T(8,128)(2,1)} %param.10) | copy-start | bytes 1572868
  6.5 138.2 %all-gather.3.cloned.1.call-start = ((), (), s32[]{:S(2)}) async-start(), calls=%async_computation.5 | async-start | bytes 10027008 | tf_op jit(solution)/shard_map/all_gather | solution.py:230
  53.4 12.5 %copy-start.5 = (s32[4,128,1]{1,2,0:T(1,128)S(1)}, s32[4,128,1]{1,2,0:T(1,128)}, u32[]{:S(2)}) copy-start(s32[4,128,1]{1,2,0:T(1,128)} %param.11) | copy-start | bytes 6148
  53.4 12.6 %copy-start.4 = (bf16[64,1024]{1,0:T(8,128)(2,1)S(1)}, bf16[64,1024]{1,0:T(8,128)(2,1)}, u32[]{:S(2)}) copy-start(bf16[64,1024]{1,0:T(8,128)(2,1)} %param.15) | copy-start | bytes 393220
  54.2 47.9 %copy-start.1 = (bf16[256,1024]{1,0:T(8,128)(2,1)S(1)}, bf16[256,1024]{1,0:T(8,128)(2,1)}, u32[]{:S(2)}) copy-start(bf16[256,1024]{1,0:T(8,128)(2,1)} %w_in_ref.1) | copy-start | bytes 1572868
  54.3 47.9 %copy-start.3 = (s32[4]{0:T(128)S(1)}, s32[4]{0:T(128)}, u32[]{:S(2)}) copy-start(s32[4]{0:T(128)} %len_ref.1) | copy-start | bytes 52
  55.3 46.7 %all-to-all-start.2 = ((bf16[512,2,256]{2,1,0:T(2,128)(2,1)}), bf16[512,2,256]{2,1,0:T(2,128)(2,1)S(1)}, u32[]{:S(2)}, u32[]{:S(2)}) async-start(bf16[512,2,256]{2,1,0:T(2,128)(2,1)} %reshape.62), calls=%async_computation.2 | async-start | bytes 1048576 | tf_op jit(solution)/shard_map/all_to_all | solution.py:251
  66.2 78.6 %copy-start.2 = (f32[2,1024]{1,0:T(2,128)S(1)}, f32[2,1024]{1,0:T(2,128)}, u32[]{:S(2)}) copy-start(f32[2,1024]{1,0:T(2,128)} %gain_ref.1) | copy-start | bytes 24580
Sparse Core Ops, SparseCore 0:
  10.4 101.8 all-gather.2

commit v3 on v2

--- a/solution.py
+++ b/solution.py
@@ -6,10 +6,11 @@
 from jax.sharding import PartitionSpec as P
 
 HEADS_STEP = 8
-INNER = 4
+INNER = 8
 MASKED = -1e30
 LOG2E = 1.4426950408889634
 EPS = 1e-06
+CAP = 2
 VMEM_BYTES = 50 * 1024 * 1024
 
 
@@ -194,26 +195,64 @@
     )(mixed, gain, weights)
 
 
-def pack_kernel(gate_ref, up_ref, down_ref, out_ref):
+def ask_kernel(
+    owner_ref, row_ref, gate_ref, up_ref, down_ref, packed_ref, request_ref, position_ref
+):
+    users, slots = owner_ref.shape
+    ntok, wide = request_ref.shape
+    owner_rows = owner_ref[...].astype(jnp.float32)
+    owner_cols, row_cols, positions = [], [], []
+    for user in range(users):
+        owner_cols.append(jnp.broadcast_to(owner_rows[user : user + 1, :], (slots, slots)).T)
+        row = row_ref[user : user + 1, :].astype(jnp.float32)
+        row_cols.append(jnp.broadcast_to(row, (slots, slots)).T[:, :1].astype(jnp.int32))
+    earlier = lax.broadcasted_iota(jnp.int32, (slots, slots), 1) < lax.broadcasted_iota(
+        jnp.int32, (slots, slots), 0
+    )
+    for user in range(users):
+        same = jnp.where(
+            earlier & (owner_cols[user] == owner_rows[user : user + 1, :]), 1.0, 0.0
+        )
+        for other in range(user):
+            same += jnp.where(owner_cols[user] == owner_rows[other : other + 1, :], 1.0, 0.0)
+        rank = jnp.sum(same, axis=1, keepdims=True)
+        positions.append((owner_cols[user][:, :1] * CAP + rank).astype(jnp.int32))
+    position = jnp.concatenate(positions, axis=0)
+    position_ref[...] = position
+    rows = jnp.concatenate(row_cols, axis=0)
+    lanes = lax.broadcasted_iota(jnp.int32, (position.shape[0], wide), 1)
+    tall = lax.broadcasted_iota(jnp.int32, (position.shape[0], ntok), 1) == position // wide
+    high = jnp.where(tall, (rows // 32).astype(jnp.float32), 0.0).astype(jnp.bfloat16)
+    low = jnp.where(tall, (rows % 32).astype(jnp.float32), 0.0).astype(jnp.bfloat16)
+    spot = jnp.where(lanes == position % wide, 1.0, 0.0).astype(jnp.bfloat16)
+    both = (((0,), (0,)), ((), ()))
+    asked_high = lax.dot_general(high, spot, both, preferred_element_type=jnp.float32)
+    asked_low = lax.dot_general(low, spot, both, preferred_element_type=jnp.float32)
+    request_ref[...] = (asked_high * 32.0 + asked_low).astype(jnp.int32)
+
     tokens, part_rows, hidden_width = gate_ref.shape
     _, down_rows, width = down_ref.shape
     rest = width - hidden_width
     extra = part_rows - down_rows
-    out_ref[:tokens] = gate_ref[...]
-    out_ref[tokens : 2 * tokens] = up_ref[...]
-    out_ref[2 * tokens :, :down_rows, :] = down_ref[:, :, :hidden_width]
+    packed_ref[:tokens] = gate_ref[...]
+    packed_ref[tokens : 2 * tokens] = up_ref[...]
+    packed_ref[2 * tokens :, :down_rows, :] = down_ref[:, :, :hidden_width]
     for piece in range(down_rows // extra):
-        out_ref[2 * tokens :, down_rows:, piece * rest : (piece + 1) * rest] = down_ref[
+        packed_ref[2 * tokens :, down_rows:, piece * rest : (piece + 1) * rest] = down_ref[
             :, piece * extra : (piece + 1) * extra, hidden_width:
         ]
 
 
-def pack_weights(w_gate, w_up, w_down):
+def ask(owners, rows, w_gate, w_up, w_down, ntok, nbatch):
     tokens, part_rows, hidden_width = w_gate.shape
     return pl.pallas_call(
-        pack_kernel,
-        out_shape=jax.ShapeDtypeStruct((3 * tokens, part_rows, hidden_width), jnp.bfloat16),
-    )(w_gate, w_up, w_down)
+        ask_kernel,
+        out_shape=[
+            jax.ShapeDtypeStruct((3 * tokens, part_rows, hidden_width), jnp.bfloat16),
+            jax.ShapeDtypeStruct((ntok, nbatch * CAP), jnp.int32),
+            jax.ShapeDtypeStruct((owners.size, 1), jnp.int32),
+        ],
+    )(owners, rows, w_gate, w_up, w_down)
 
 
 def shards(table, hist_owner, hist_row, hist_len, w_in, queries, ffn_gain, w_gate, w_up, w_down):
@@ -225,20 +264,12 @@
     width = w_in.shape[1]
     nquery = queries.shape[0]
     headsz = width // nquery
-    count = users * slots
-    cap = 2 * count // devices
-    weights = lax.all_gather(pack_weights(w_gate, w_up, w_down)[None], "batch", axis=0, tiled=True)
-
-    owners = hist_owner.reshape(count)
-    places = jnp.arange(count, dtype=jnp.int32)
-    same = (owners[:, None] == owners[None, :]) & (places[None, :] < places[:, None])
-    rank = jnp.sum(same.astype(jnp.int32), axis=1)
-    position = owners * cap + rank
-    spots = jnp.arange(devices * cap, dtype=jnp.int32)
-    request = jnp.sum(
-        jnp.where(position[:, None] == spots[None, :], hist_row.reshape(count)[:, None], 0), axis=0
-    )
-    asked = lax.all_to_all(request.reshape(ntok, nbatch * cap), "tok", 0, 0, tiled=True)
+    cap = CAP
+    packed, request, position = ask(
+        hist_owner.reshape(users, slots), hist_row, w_gate, w_up, w_down, ntok, nbatch
+    )
+    weights = lax.all_gather(packed[None], "batch", axis=0, tiled=True)
+    asked = lax.all_to_all(request, "tok", 0, 0, tiled=True)
     asked = asked.reshape(ntok, nbatch, cap).transpose(1, 0, 2).reshape(nbatch, ntok * cap)
     asked = lax.all_to_all(asked, "batch", 0, 0, tiled=True)
     wanted = asked.reshape(nbatch, ntok, cap).transpose(1, 0, 2).reshape(devices * cap)
@@ -251,7 +282,7 @@
     answers = lax.all_to_all(
         served.reshape(devices, cap, emb), ("tok", "batch"), 0, 0, tiled=True
     ).reshape(devices * cap, emb)
-    pooled = pool(hist_len, answers, position.reshape(count, 1), w_in, queries)
+    pooled = pool(hist_len, answers, position, w_in, queries)
     mixed = lax.all_to_all(pooled, "tok", 0, 0, tiled=True)
     group = users * ntok
     tokens = nquery // ntok

time: 194 us -> 192 us (0.990)
  other arithmetic: 2.66 us -> 0 us
    reduce_sum x2 -> x0, other arithmetic: 1.97 us -> none  [the longest x1 1 us: shards(): rank = jnp.sum(same.astype(jnp.int32), axis=1)]
  transfers between devices with their start and end apart: 2 -> 2, of which waited for: 1 -> 1; matrix products, arithmetic and copies ran while one was open for 3% -> 2% of each run, Pallas kernels for 3% -> 3%
where the time goes in v3:
time: 192 us
  blocking collectives  115 us (60%)
  waiting for transfers between devices  35.9 us (19%)
  between operations  13.5 us (7%)
  Pallas kernels  12.4 us (6%)
  starting transfers between devices  10.6 us (6%)
  local copies, waits for them, and re-layouts  3.28 us (2%)
    all_to_all x1, blocking collectives, shards(): back = lax.all_to_all(sent, 'tok', 0, 0, tiled=True)  37 us
    all_to_all x1, blocking collectives, shards(): mixed = lax.all_to_all(pooled, 'tok', 0, 0, tiled=True)  36.9 us
    all_to_all x1, waiting for transfers between devices, shards(): lax.all_to_all(served.reshape(devices, cap, emb), ('tok', 'batch'), 0, 0,...  35.9 us
    all_to_all x1, blocking collectives, shards(): asked = lax.all_to_all(request, 'tok', 0, 0, tiled=True)  28.6 us
    all_to_all x1, blocking collectives, shards(): asked = lax.all_to_all(asked, 'batch', 0, 0, tiled=True)  13 us
    all_to_all x1, starting transfers between devices, shards(): lax.all_to_all(served.reshape(devices, cap, emb), ('tok', 'batch'), 0, 0,...  10.6 us
    pallas_call x1, Pallas kernels, pool(): pl.pallas_call(pool_kernel, grid=(parts // INNER,), in_specs=[pl.BlockSpe...  5.03 us
    pallas_call x1, Pallas kernels, net(): pl.pallas_call(net_kernel, in_specs=[pl.BlockSpec(memory_space=pltpu.VMEM...  4.31 us
  transfers between devices with their start and end apart: 2, of which 1 were waited for; matrix products, arithmetic and copies ran while one was open for 2% of the time, Pallas kernels for 3%

profile of v3, /device:TPU:1, one launch (start us, length us, event | category | flops | bytes accessed | tf_op | source)
XLA Modules:
  0.0 191.9 jit_solution(13064677568856301865)
XLA Ops:
  6.5 0.0 copy-start
  6.5 0.0 copy-start.5
  6.5 0.0 all-gather.3.cloned.1.call-start
  6.5 3.0 %shard_map.100 = (bf16[6,64,768]{2,1,0:T(8,128)(2,1)}, s32[32,32]{1,0:T(8,128)}, s32[512,1]{1,0:T(8,128)}) custom-call(s32[4,128]{1,0:T(4,128)} %bitcast.28, s32[4,128]{1,0:T(4,128)} %row_ref.1, bf16[2,64,768]{2,1,0:T(8,128)(2,1)} %gate_ref.1, bf16[2,64,768]{2,1,0:T(8,128)(2,1)} %up_ref.1, bf16[2,48,1024]{2,1,0:T(8,128)(2,1)} %down_ref.1), custom_call_target="tpu_custom_call" | custom-call | tf_op jit(solution)/shard_map/pallas_call | solution.py:248
  9.6 0.0 copy-start.1
  9.6 0.0 all-gather.3.cloned.1.call-update
  9.6 28.6 %all_to_all.33 = s32[32,1,32]{2,1,0:T(1,128)S(1)} all-to-all(s32[32,1,32]{2,1,0:T(1,128)} %bitcast.27), channel_id=1, replica_groups=mesh['tok'=32,'batch'=16] {'tok'}, dimensions={0} | all-to-all | bytes 8192 | tf_op jit(solution)/shard_map/all_to_all | solution.py:272
  38.2 0.1 copy.19
  38.3 0.1 copy.20
  38.4 0.1 copy.21
  38.4 13.0 %all_to_all.34 = s32[16,1,64]{2,1,0:T(1,128)S(1)} all-to-all(s32[16,1,64]{2,1,0:T(1,128)S(1)} %copy.21), channel_id=1, replica_groups=mesh['tok'=32,'batch'=16] {'batch'}, dimensions={0} | all-to-all | bytes 8192 | tf_op jit(solution)/shard_map/all_to_all | solution.py:274
  51.4 0.1 copy.22
  51.5 0.3 copy.23
  51.8 0.2 eq.15
  51.9 0.0 copy-done
  51.9 0.8 fusion
  52.8 0.0 copy-start.3
  52.8 1.0 reshape.36
  53.8 10.6 %all-to-all-start.2 = ((bf16[512,2,256]{2,1,0:T(2,128)(2,1)}), bf16[512,2,256]{2,1,0:T(2,128)(2,1)S(1)}, u32[]{:S(2)}, u32[]{:S(2)}) async-start(bf16[512,2,256]{2,1,0:T(2,128)(2,1)} %reshape.36), calls=%async_computation.2 | async-start | bytes 1048576 | tf_op jit(solution)/shard_map/all_to_all | solution.py:282
  64.3 0.0 copy-done.5
  64.4 0.2 copy.24
  64.5 35.9 %all-to-all-done.2 = bf16[512,2,256]{2,1,0:T(2,128)(2,1)S(1)} async-done(((bf16[512,2,256]{2,1,0:T(2,128)(2,1)}), bf16[512,2,256]{2,1,0:T(2,128)(2,1)S(1)}, u32[]{:S(2)}, u32[]{:S(2)}) %all-to-all-start.2) | async-done | bytes 524320 | tf_op jit(solution)/shard_map/all_to_all | solution.py:282
  100.4 0.2 reshape.37.answer_ref
  100.6 0.0 copy-done.1
  100.6 0.0 copy-done.2
  100.6 0.0 copy-done.4
  100.7 5.0 %shard_map.101 = bf16[32,8,1024]{2,1,0:T(8,128)(2,1)S(1)} custom-call(s32[4]{0:T(128)S(1)} %copy-done.4, bf16[1024,256]{1,0:T(8,128)(2,1)S(1)} %reshape.37.answer_ref, s32[512,1]{1,0:T(8,128)S(1)} %copy-done.2, bf16[256,1024]{1,0:T(8,128)(2,1)S(1)} %copy-done.1, bf16[8,128,64]{2,1,0:T(8,128)(2,1)S(1)} %bitcast.19), custom_call_target="tpu_custom_call" | custom-call | tf_op jit(solution)/shard_map/pallas_call | solution.py:90
  105.7 36.9 %all_to_all.35 = bf16[32,8,1024]{2,1,0:T(8,128)(2,1)S(1)} all-to-all(bf16[32,8,1024]{2,1,0:T(8,128)(2,1)S(1)} %shard_map.101), channel_id=1, replica_groups=mesh['tok'=32,'batch'=16] {'tok'}, dimensions={0} | all-to-all | bytes 1048576 | tf_op jit(solution)/shard_map/all_to_all | solution.py:286
  142.6 0.0 copy-done.3
  142.6 4.3 %shard_map.102 = bf16[32,2,2,16,128]{4,3,2,1,0:T(8,128)(2,1)S(1)} custom-call(bf16[256,1024]{1,0:T(8,128)(2,1)S(1)} %bitcast.18, f32[2,1024]{1,0:T(2,128)S(1)} %copy-done.3, bf16[16,6,64,768]{3,2,1,0:T(8,128)(2,1)} %bitcast.20), custom_call_target="tpu_custom_call" | custom-call | tf_op jit(solution)/shard_map/pallas_call | solution.py:177
  146.9 37.0 %all_to_all.36 = bf16[32,2,2,16,128]{4,3,2,1,0:T(8,128)(2,1)S(1)} all-to-all(bf16[32,2,2,16,128]{4,3,2,1,0:T(8,128)(2,1)S(1)} %shard_map.102), channel_id=1, replica_groups=mesh['tok'=32,'batch'=16] {'tok'}, dimensions={0} | all-to-all | bytes 1048576 | tf_op jit(solution)/shard_map/all_to_all | solution.py:290
  184.0 1.1 copy.26
  (4 shorter events, 0.0 us)
Async XLA Ops:
  6.5 45.4 %copy-start = (bf16[1024,256]{1,0:T(8,128)(2,1)S(1)}, bf16[1024,256]{1,0:T(8,128)(2,1)}, u32[]{:S(2)}) copy-start(bf16[1024,256]{1,0:T(8,128)(2,1)} %param.10) | copy-start | bytes 1572868
  6.5 57.8 %copy-start.5 = (bf16[64,1024]{1,0:T(8,128)(2,1)S(1)}, bf16[64,1024]{1,0:T(8,128)(2,1)}, u32[]{:S(2)}) copy-start(bf16[64,1024]{1,0:T(8,128)(2,1)} %param.15) | copy-start | bytes 393220
  6.5 136.1 %all-gather.3.cloned.1.call-start = ((), (), s32[]{:S(2)}) async-start(), calls=%async_computation.5 | async-start | bytes 10027008 | tf_op jit(solution)/shard_map/all_gather | solution.py:271
  9.6 91.1 %copy-start.1 = (bf16[256,1024]{1,0:T(8,128)(2,1)S(1)}, bf16[256,1024]{1,0:T(8,128)(2,1)}, u32[]{:S(2)}) copy-start(bf16[256,1024]{1,0:T(8,128)(2,1)} %w_in_ref.1) | copy-start | bytes 1572868
  9.6 91.1 %copy-start.2 = (s32[512,1]{1,0:T(8,128)S(1)}, s32[512,1]{1,0:T(8,128)}, u32[]{:S(2)}) copy-start(s32[512,1]{1,0:T(8,128)} %get-tuple-element.9.position_ref) | copy-start | bytes 6148
  9.6 91.1 %copy-start.4 = (s32[4]{0:T(128)S(1)}, s32[4]{0:T(128)}, u32[]{:S(2)}) copy-start(s32[4]{0:T(128)} %len_ref.1) | copy-start | bytes 52
  52.8 89.9 %copy-start.3 = (f32[2,1024]{1,0:T(2,128)S(1)}, f32[2,1024]{1,0:T(2,128)}, u32[]{:S(2)}) copy-start(f32[2,1024]{1,0:T(2,128)} %gain_ref.1) | copy-start | bytes 24580
  53.8 46.6 %all-to-all-start.2 = ((bf16[512,2,256]{2,1,0:T(2,128)(2,1)}), bf16[512,2,256]{2,1,0:T(2,128)(2,1)S(1)}, u32[]{:S(2)}, u32[]{:S(2)}) async-start(bf16[512,2,256]{2,1,0:T(2,128)(2,1)} %reshape.36), calls=%async_computation.2 | async-start | bytes 1048576 | tf_op jit(solution)/shard_map/all_to_all | solution.py:282
Sparse Core Ops, SparseCore 0:
  10.4 101.8 all-gather.2

commit v4 on v3

--- a/solution.py
+++ b/solution.py
@@ -25,7 +25,7 @@
 
 def pool_kernel(len_ref, answer_ref, position_ref, w_in_ref, query_ref, out_ref, keys_ref):
     users = len_ref.shape[0]
-    slots = position_ref.shape[0] // users
+    slots = position_ref.shape[1]
     inner, step_width, nquery = query_ref.shape
     headsz = step_width // HEADS_STEP
     heads = HEADS_STEP // 2
@@ -33,9 +33,11 @@
 
     @pl.when(step == 0)
     def _():
+        placed = position_ref[...].astype(jnp.float32)
+        columns = jnp.concatenate([placed, placed], axis=0).T.astype(jnp.int32)
         for user in range(users):
             span = slice(user * slots, (user + 1) * slots)
-            pick = one_hot(position_ref[span, :], answer_ref.shape[0])
+            pick = one_hot(columns[:, user : user + 1], answer_ref.shape[0])
             rows = dot32(pick, answer_ref[...]).astype(jnp.bfloat16)
             proj = dot32(rows, w_in_ref[...])
             scale = lax.rsqrt(jnp.mean(proj * proj, axis=-1, keepdims=True) + EPS)
@@ -99,7 +101,7 @@
         ],
         out_specs=pl.BlockSpec((INNER * HEADS_STEP // 2, 2 * users, width), lambda i: (i, 0, 0)),
         out_shape=jax.ShapeDtypeStruct((pairs, 2 * users, width), jnp.bfloat16),
-        scratch_shapes=[pltpu.VMEM((parts, position.shape[0], step_width), jnp.bfloat16)],
+        scratch_shapes=[pltpu.VMEM((parts, position.size, step_width), jnp.bfloat16)],
         compiler_params=pltpu.CompilerParams(vmem_limit_bytes=VMEM_BYTES),
     )(lengths, answers, position, w_in, query_t)
 
@@ -201,34 +203,33 @@
     users, slots = owner_ref.shape
     ntok, wide = request_ref.shape
     owner_rows = owner_ref[...].astype(jnp.float32)
-    owner_cols, row_cols, positions = [], [], []
+    owner_cols = jnp.concatenate([owner_rows, owner_rows], axis=0).T
+    earlier = lax.broadcasted_iota(jnp.int32, (slots, slots), 0) < lax.broadcasted_iota(
+        jnp.int32, (slots, slots), 1
+    )
+    lanes = lax.broadcasted_iota(jnp.int32, (wide, slots), 0)
+    groups = lax.broadcasted_iota(jnp.int32, (ntok, slots), 0)
+    across = (((1,), (1,)), ((), ()))
+    asked = jnp.zeros((ntok, wide), jnp.float32)
+    positions = []
     for user in range(users):
-        owner_cols.append(jnp.broadcast_to(owner_rows[user : user + 1, :], (slots, slots)).T)
-        row = row_ref[user : user + 1, :].astype(jnp.float32)
-        row_cols.append(jnp.broadcast_to(row, (slots, slots)).T[:, :1].astype(jnp.int32))
-    earlier = lax.broadcasted_iota(jnp.int32, (slots, slots), 1) < lax.broadcasted_iota(
-        jnp.int32, (slots, slots), 0
-    )
-    for user in range(users):
-        same = jnp.where(
-            earlier & (owner_cols[user] == owner_rows[user : user + 1, :]), 1.0, 0.0
-        )
+        mine = owner_rows[user : user + 1, :]
+        same = jnp.where(earlier & (owner_cols[:, user : user + 1] == mine), 1.0, 0.0)
         for other in range(user):
-            same += jnp.where(owner_cols[user] == owner_rows[other : other + 1, :], 1.0, 0.0)
-        rank = jnp.sum(same, axis=1, keepdims=True)
-        positions.append((owner_cols[user][:, :1] * CAP + rank).astype(jnp.int32))
-    position = jnp.concatenate(positions, axis=0)
-    position_ref[...] = position
-    rows = jnp.concatenate(row_cols, axis=0)
-    lanes = lax.broadcasted_iota(jnp.int32, (position.shape[0], wide), 1)
-    tall = lax.broadcasted_iota(jnp.int32, (position.shape[0], ntok), 1) == position // wide
-    high = jnp.where(tall, (rows // 32).astype(jnp.float32), 0.0).astype(jnp.bfloat16)
-    low = jnp.where(tall, (rows % 32).astype(jnp.float32), 0.0).astype(jnp.bfloat16)
-    spot = jnp.where(lanes == position % wide, 1.0, 0.0).astype(jnp.bfloat16)
-    both = (((0,), (0,)), ((), ()))
-    asked_high = lax.dot_general(high, spot, both, preferred_element_type=jnp.float32)
-    asked_low = lax.dot_general(low, spot, both, preferred_element_type=jnp.float32)
-    request_ref[...] = (asked_high * 32.0 + asked_low).astype(jnp.int32)
+            same += jnp.where(owner_cols[:, other : other + 1] == mine, 1.0, 0.0)
+        rank = jnp.sum(same, axis=0, keepdims=True)
+        position = (mine * CAP + rank).astype(jnp.int32)
+        positions.append(position)
+        row = row_ref[user : user + 1, :]
+        here = groups == position // wide
+        high = jnp.where(here, (row // 32).astype(jnp.float32), 0.0).astype(jnp.bfloat16)
+        low = jnp.where(here, (row % 32).astype(jnp.float32), 0.0).astype(jnp.bfloat16)
+        spot = jnp.where(lanes == position % wide, 1.0, 0.0).astype(jnp.bfloat16)
+        asked_high = lax.dot_general(high, spot, across, preferred_element_type=jnp.float32)
+        asked_low = lax.dot_general(low, spot, across, preferred_element_type=jnp.float32)
+        asked += asked_high * 32.0 + asked_low
+    position_ref[...] = jnp.concatenate(positions, axis=0)
+    request_ref[...] = asked.astype(jnp.int32)
 
     tokens, part_rows, hidden_width = gate_ref.shape
     _, down_rows, width = down_ref.shape
@@ -250,7 +251,7 @@
         out_shape=[
             jax.ShapeDtypeStruct((3 * tokens, part_rows, hidden_width), jnp.bfloat16),
             jax.ShapeDtypeStruct((ntok, nbatch * CAP), jnp.int32),
-            jax.ShapeDtypeStruct((owners.size, 1), jnp.int32),
+            jax.ShapeDtypeStruct(owners.shape, jnp.int32),
         ],
     )(owners, rows, w_gate, w_up, w_down)
 

time: 192 us -> 192 us (level)
  no operation moved by 1% of the time
where the time goes in v4:
time: 192 us; the launch traced here: 191 us
  blocking collectives  116 us (60%)
  waiting for transfers between devices  35.9 us (19%)
  between operations  13.5 us (7%)
  Pallas kernels  11.8 us (6%)
  starting transfers between devices  10.6 us (6%)
  local copies, waits for them, and re-layouts  3.28 us (2%)
    all_to_all x1, blocking collectives, shards(): back = lax.all_to_all(sent, 'tok', 0, 0, tiled=True)  37 us
    all_to_all x1, blocking collectives, shards(): mixed = lax.all_to_all(pooled, 'tok', 0, 0, tiled=True)  36.9 us
    all_to_all x1, waiting for transfers between devices, shards(): lax.all_to_all(served.reshape(devices, cap, emb), ('tok', 'batch'), 0, 0,...  35.9 us
    all_to_all x1, blocking collectives, shards(): asked = lax.all_to_all(request, 'tok', 0, 0, tiled=True)  28.6 us
    all_to_all x1, blocking collectives, shards(): asked = lax.all_to_all(asked, 'batch', 0, 0, tiled=True)  13 us
    all_to_all x1, starting transfers between devices, shards(): lax.all_to_all(served.reshape(devices, cap, emb), ('tok', 'batch'), 0, 0,...  10.6 us
    pallas_call x1, Pallas kernels, pool(): pl.pallas_call(pool_kernel, grid=(parts // INNER,), in_specs=[pl.BlockSpe...  5.1 us
    pallas_call x1, Pallas kernels, net(): pl.pallas_call(net_kernel, in_specs=[pl.BlockSpec(memory_space=pltpu.VMEM...  4.3 us
  transfers between devices with their start and end apart: 2, of which 1 were waited for; matrix products, arithmetic and copies ran while one was open for 2% of the time, Pallas kernels for 3%

profile of v4, /device:TPU:1, one launch (start us, length us, event | category | flops | bytes accessed | tf_op | source)
XLA Modules:
  0.0 191.3 jit_solution(11568345609122219293)
XLA Ops:
  6.5 0.0 copy-start
  6.5 0.0 copy-start.5
  6.5 0.0 all-gather.3.cloned.1.call-start
  6.5 2.4 %shard_map.100 = (bf16[6,64,768]{2,1,0:T(8,128)(2,1)}, s32[32,32]{1,0:T(8,128)}, s32[4,128]{1,0:T(4,128)}) custom-call(s32[4,128]{1,0:T(4,128)} %bitcast.28, s32[4,128]{1,0:T(4,128)} %row_ref.1, bf16[2,64,768]{2,1,0:T(8,128)(2,1)} %gate_ref.1, bf16[2,64,768]{2,1,0:T(8,128)(2,1)} %up_ref.1, bf16[2,48,1024]{2,1,0:T(8,128)(2,1)} %down_ref.1), custom_call_target="tpu_custom_call" | custom-call | tf_op jit(solution)/shard_map/pallas_call | solution.py:249
  8.9 0.0 copy-start.1
  8.9 0.0 all-gather.3.cloned.1.call-update
  8.9 28.6 %all_to_all.33 = s32[32,1,32]{2,1,0:T(1,128)S(1)} all-to-all(s32[32,1,32]{2,1,0:T(1,128)} %bitcast.27), channel_id=1, replica_groups=mesh['tok'=32,'batch'=16] {'tok'}, dimensions={0} | all-to-all | bytes 8192 | tf_op jit(solution)/shard_map/all_to_all | solution.py:273
  37.5 0.1 copy.19
  37.6 0.1 copy.20
  37.7 0.1 copy.21
  37.8 13.0 %all_to_all.34 = s32[16,1,64]{2,1,0:T(1,128)S(1)} all-to-all(s32[16,1,64]{2,1,0:T(1,128)S(1)} %copy.21), channel_id=1, replica_groups=mesh['tok'=32,'batch'=16] {'batch'}, dimensions={0} | all-to-all | bytes 8192 | tf_op jit(solution)/shard_map/all_to_all | solution.py:275
  50.7 0.1 copy.22
  50.8 0.3 copy.23
  51.1 0.2 eq.15
  51.2 0.0 copy-done
  51.3 0.0 copy-start.2
  51.3 0.8 fusion
  52.1 1.0 reshape.36
  53.1 10.6 %all-to-all-start.2 = ((bf16[512,2,256]{2,1,0:T(2,128)(2,1)}), bf16[512,2,256]{2,1,0:T(2,128)(2,1)S(1)}, u32[]{:S(2)}, u32[]{:S(2)}) async-start(bf16[512,2,256]{2,1,0:T(2,128)(2,1)} %reshape.36), calls=%async_computation.2 | async-start | bytes 1048576 | tf_op jit(solution)/shard_map/all_to_all | solution.py:283
  63.7 0.0 copy-done.5
  63.7 0.2 copy.24
  63.9 35.9 %all-to-all-done.2 = bf16[512,2,256]{2,1,0:T(2,128)(2,1)S(1)} async-done(((bf16[512,2,256]{2,1,0:T(2,128)(2,1)}), bf16[512,2,256]{2,1,0:T(2,128)(2,1)S(1)}, u32[]{:S(2)}, u32[]{:S(2)}) %all-to-all-start.2) | async-done | bytes 524320 | tf_op jit(solution)/shard_map/all_to_all | solution.py:283
  99.8 0.2 reshape.37.answer_ref
  100.0 0.0 copy-done.1
  100.0 0.0 copy-done.3
  100.0 0.0 copy-done.4
  100.0 5.1 %shard_map.101 = bf16[32,8,1024]{2,1,0:T(8,128)(2,1)S(1)} custom-call(s32[4]{0:T(128)S(1)} %copy-done.4, bf16[1024,256]{1,0:T(8,128)(2,1)S(1)} %reshape.37.answer_ref, s32[4,128]{1,0:T(4,128)S(1)} %copy-done.3, bf16[256,1024]{1,0:T(8,128)(2,1)S(1)} %copy-done.1, bf16[8,128,64]{2,1,0:T(8,128)(2,1)S(1)} %bitcast.19), custom_call_target="tpu_custom_call" | custom-call | tf_op jit(solution)/shard_map/pallas_call | solution.py:92
  105.1 36.9 %all_to_all.35 = bf16[32,8,1024]{2,1,0:T(8,128)(2,1)S(1)} all-to-all(bf16[32,8,1024]{2,1,0:T(8,128)(2,1)S(1)} %shard_map.101), channel_id=1, replica_groups=mesh['tok'=32,'batch'=16] {'tok'}, dimensions={0} | all-to-all | bytes 1048576 | tf_op jit(solution)/shard_map/all_to_all | solution.py:287
  142.0 0.0 copy-done.2
  142.0 4.3 %shard_map.102 = bf16[32,2,2,16,128]{4,3,2,1,0:T(8,128)(2,1)S(1)} custom-call(bf16[256,1024]{1,0:T(8,128)(2,1)S(1)} %bitcast.18, f32[2,1024]{1,0:T(2,128)S(1)} %copy-done.2, bf16[16,6,64,768]{3,2,1,0:T(8,128)(2,1)} %bitcast.20), custom_call_target="tpu_custom_call" | custom-call | tf_op jit(solution)/shard_map/pallas_call | solution.py:179
  146.3 37.0 %all_to_all.36 = bf16[32,2,2,16,128]{4,3,2,1,0:T(8,128)(2,1)S(1)} all-to-all(bf16[32,2,2,16,128]{4,3,2,1,0:T(8,128)(2,1)S(1)} %shard_map.102), channel_id=1, replica_groups=mesh['tok'=32,'batch'=16] {'tok'}, dimensions={0} | all-to-all | bytes 1048576 | tf_op jit(solution)/shard_map/all_to_all | solution.py:291
  183.4 1.1 copy.26
  (4 shorter events, 0.0 us)
Async XLA Ops:
  6.5 44.7 %copy-start = (bf16[1024,256]{1,0:T(8,128)(2,1)S(1)}, bf16[1024,256]{1,0:T(8,128)(2,1)}, u32[]{:S(2)}) copy-start(bf16[1024,256]{1,0:T(8,128)(2,1)} %param.10) | copy-start | bytes 1572868
  6.5 57.1 %copy-start.5 = (bf16[64,1024]{1,0:T(8,128)(2,1)S(1)}, bf16[64,1024]{1,0:T(8,128)(2,1)}, u32[]{:S(2)}) copy-start(bf16[64,1024]{1,0:T(8,128)(2,1)} %param.15) | copy-start | bytes 393220
  6.5 135.5 %all-gather.3.cloned.1.call-start = ((), (), s32[]{:S(2)}) async-start(), calls=%async_computation.5 | async-start | bytes 10027008 | tf_op jit(solution)/shard_map/all_gather | solution.py:272
  8.9 91.1 %copy-start.1 = (bf16[256,1024]{1,0:T(8,128)(2,1)S(1)}, bf16[256,1024]{1,0:T(8,128)(2,1)}, u32[]{:S(2)}) copy-start(bf16[256,1024]{1,0:T(8,128)(2,1)} %w_in_ref.1) | copy-start | bytes 1572868
  8.9 91.1 %copy-start.3 = (s32[4,128]{1,0:T(4,128)S(1)}, s32[4,128]{1,0:T(4,128)}, u32[]{:S(2)}) copy-start(s32[4,128]{1,0:T(4,128)} %get-tuple-element.9.position_ref) | copy-start | bytes 6148
  8.9 91.1 %copy-start.4 = (s32[4]{0:T(128)S(1)}, s32[4]{0:T(128)}, u32[]{:S(2)}) copy-start(s32[4]{0:T(128)} %len_ref.1) | copy-start | bytes 52
  51.3 90.8 %copy-start.2 = (f32[2,1024]{1,0:T(2,128)S(1)}, f32[2,1024]{1,0:T(2,128)}, u32[]{:S(2)}) copy-start(f32[2,1024]{1,0:T(2,128)} %gain_ref.1) | copy-start | bytes 24580
  53.1 46.6 %all-to-all-start.2 = ((bf16[512,2,256]{2,1,0:T(2,128)(2,1)}), bf16[512,2,256]{2,1,0:T(2,128)(2,1)S(1)}, u32[]{:S(2)}, u32[]{:S(2)}) async-start(bf16[512,2,256]{2,1,0:T(2,128)(2,1)} %reshape.36), calls=%async_computation.2 | async-start | bytes 1048576 | tf_op jit(solution)/shard_map/all_to_all | solution.py:283
Sparse Core Ops, SparseCore 0:
  10.4 101.7 all-gather.2

commit v5 on v4

--- a/solution.py
+++ b/solution.py
@@ -106,40 +106,26 @@
     )(lengths, answers, position, w_in, query_t)
 
 
-def net_kernel(mixed_ref, gain_ref, weight_ref, out_ref, gate_ref, up_ref, down_ref, sems):
+def net_kernel(mixed_ref, gain_ref, weight_ref, out_ref, held_ref, sems):
     tokens = gain_ref.shape[0]
     rows, width = mixed_ref.shape
     group = rows // tokens
-    nparts, _, part_rows, hidden_width = weight_ref.shape
-    down_rows = down_ref.shape[2]
+    _, nparts, _, part_rows, hidden_width = held_ref.shape
+    down_rows = hidden_width // nparts
     rest = width - hidden_width
+    extra = part_rows - down_rows
     headsz = out_ref.shape[3]
-    copies = []
-    for token in range(tokens):
-        pieces = [
-            (weight_ref.at[:, token, :, :], gate_ref.at[token]),
-            (weight_ref.at[:, tokens + token, :, :], up_ref.at[token]),
-            (
-                weight_ref.at[:, 2 * tokens + token, pl.ds(0, down_rows), :],
-                down_ref.at[token, :, :, pl.ds(0, hidden_width)],
-            ),
+    copies = [
+        [
+            pltpu.make_async_copy(
+                weight_ref.at[:, token, pl.ds(first, some)],
+                held_ref.at[token, :, pl.ds(first, some)],
+                sems.at[token, number],
+            )
+            for number, (first, some) in enumerate(((0, 2), (2, 1)))
         ]
-        extra = part_rows - down_rows
-        for piece in range(down_rows // extra):
-            pieces.append(
-                (
-                    weight_ref.at[
-                        :, 2 * tokens + token, pl.ds(down_rows, extra), pl.ds(piece * rest, rest)
-                    ],
-                    down_ref.at[token, :, pl.ds(piece * extra, extra), pl.ds(hidden_width, rest)],
-                )
-            )
-        copies.append(
-            [
-                pltpu.make_async_copy(src, dst, sems.at[token, number])
-                for number, (src, dst) in enumerate(pieces)
-            ]
-        )
+        for token in range(tokens)
+    ]
     for some in copies:
         for copy in some:
             copy.start()
@@ -155,13 +141,19 @@
         scale = lax.rsqrt(jnp.mean(wide * wide, axis=-1, keepdims=True) + EPS)
         normed = (wide * scale * gain_ref[token : token + 1, :]).astype(jnp.bfloat16)
         copies[token][0].wait()
-        gate = dot32(normed, gate_ref[token].reshape(width, hidden_width))
+        gate = dot32(normed, held_ref[token, :, 0].reshape(width, hidden_width))
+        up_val = dot32(normed, held_ref[token, :, 1].reshape(width, hidden_width))
+        hidden = (gate / (1.0 + jnp.exp(-gate)) * up_val).astype(jnp.bfloat16)
         copies[token][1].wait()
-        up_val = dot32(normed, up_ref[token].reshape(width, hidden_width))
-        hidden = (gate / (1.0 + jnp.exp(-gate)) * up_val).astype(jnp.bfloat16)
-        for copy in copies[token][2:]:
-            copy.wait()
-        down = dot32(hidden, down_ref[token].reshape(hidden_width, width))
+        left = held_ref[token, :, 2, :down_rows, :].reshape(hidden_width, hidden_width)
+        right = jnp.stack(
+            [
+                held_ref[token, :, 2, down_rows:, piece * rest : (piece + 1) * rest]
+                for piece in range(down_rows // extra)
+            ],
+            axis=1,
+        ).reshape(hidden_width, rest)
+        down = jnp.concatenate([dot32(hidden, left), dot32(hidden, right)], axis=1)
         summed = (wide + down).T.astype(jnp.bfloat16)
         out_ref[:, :, token, :, :] = summed.reshape(
             out_ref.shape[0], out_ref.shape[1], headsz, group
@@ -172,10 +164,8 @@
     rows, width = mixed.shape
     tokens = gain.shape[0]
     group = rows // tokens
-    nparts, _, part_rows, hidden_width = weights.shape
-    down_rows = hidden_width // nparts
+    nparts, _, kinds, part_rows, hidden_width = weights.shape
     nquery = ntok * tokens
-    pieces = 3 + down_rows // (part_rows - down_rows)
     return pl.pallas_call(
         net_kernel,
         in_specs=[
@@ -188,10 +178,8 @@
             (ntok, tokens, tokens, width // nquery, group), jnp.bfloat16
         ),
         scratch_shapes=[
-            pltpu.VMEM((tokens, nparts, part_rows, hidden_width), jnp.bfloat16),
-            pltpu.VMEM((tokens, nparts, part_rows, hidden_width), jnp.bfloat16),
-            pltpu.VMEM((tokens, nparts, down_rows, width), jnp.bfloat16),
-            pltpu.SemaphoreType.DMA((tokens, pieces)),
+            pltpu.VMEM((tokens, nparts, kinds, part_rows, hidden_width), jnp.bfloat16),
+            pltpu.SemaphoreType.DMA((tokens, 2)),
         ],
         compiler_params=pltpu.CompilerParams(vmem_limit_bytes=VMEM_BYTES),
     )(mixed, gain, weights)
@@ -235,13 +223,14 @@
     _, down_rows, width = down_ref.shape
     rest = width - hidden_width
     extra = part_rows - down_rows
-    packed_ref[:tokens] = gate_ref[...]
-    packed_ref[tokens : 2 * tokens] = up_ref[...]
-    packed_ref[2 * tokens :, :down_rows, :] = down_ref[:, :, :hidden_width]
-    for piece in range(down_rows // extra):
-        packed_ref[2 * tokens :, down_rows:, piece * rest : (piece + 1) * rest] = down_ref[
-            :, piece * extra : (piece + 1) * extra, hidden_width:
-        ]
+    for token in range(tokens):
+        packed_ref[token, 0] = gate_ref[token]
+        packed_ref[token, 1] = up_ref[token]
+        packed_ref[token, 2, :down_rows, :] = down_ref[token, :, :hidden_width]
+        for piece in range(down_rows // extra):
+            packed_ref[token, 2, down_rows:, piece * rest : (piece + 1) * rest] = down_ref[
+                token, piece * extra : (piece + 1) * extra, hidden_width:
+            ]
 
 
 def ask(owners, rows, w_gate, w_up, w_down, ntok, nbatch):
@@ -249,7 +238,7 @@
     return pl.pallas_call(
         ask_kernel,
         out_shape=[
-            jax.ShapeDtypeStruct((3 * tokens, part_rows, hidden_width), jnp.bfloat16),
+            jax.ShapeDtypeStruct((tokens, 3, part_rows, hidden_width), jnp.bfloat16),
             jax.ShapeDtypeStruct((ntok, nbatch * CAP), jnp.int32),
             jax.ShapeDtypeStruct(owners.shape, jnp.int32),
         ],

time: 192 us -> 192 us (level)
  no operation moved by 1% of the time
where the time goes in v5:
time: 192 us
  blocking collectives  115 us (60%)
  waiting for transfers between devices  35.9 us (19%)
  between operations  13.5 us (7%)
  Pallas kernels  12 us (6%)
  starting transfers between devices  10.6 us (6%)
  local copies, waits for them, and re-layouts  3.28 us (2%)
    all_to_all x1, blocking collectives, shards(): back = lax.all_to_all(sent, 'tok', 0, 0, tiled=True)  37 us
    all_to_all x1, blocking collectives, shards(): mixed = lax.all_to_all(pooled, 'tok', 0, 0, tiled=True)  36.9 us
    all_to_all x1, waiting for transfers between devices, shards(): lax.all_to_all(served.reshape(devices, cap, emb), ('tok', 'batch'), 0, 0,...  35.9 us
    all_to_all x1, blocking collectives, shards(): asked = lax.all_to_all(request, 'tok', 0, 0, tiled=True)  28.6 us
    all_to_all x1, blocking collectives, shards(): asked = lax.all_to_all(asked, 'batch', 0, 0, tiled=True)  13 us
    all_to_all x1, starting transfers between devices, shards(): lax.all_to_all(served.reshape(devices, cap, emb), ('tok', 'batch'), 0, 0,...  10.6 us
    pallas_call x1, Pallas kernels, pool(): pl.pallas_call(pool_kernel, grid=(parts // INNER,), in_specs=[pl.BlockSpe...  5.1 us
    pallas_call x1, Pallas kernels, net(): pl.pallas_call(net_kernel, in_specs=[pl.BlockSpec(memory_space=pltpu.VMEM...  4.5 us
  transfers between devices with their start and end apart: 2, of which 1 were waited for; matrix products, arithmetic and copies ran while one was open for 2% of the time, Pallas kernels for 3%

profile of v5, /device:TPU:1, one launch (start us, length us, event | category | flops | bytes accessed | tf_op | source)
XLA Modules:
  0.0 191.5 jit_solution(18138705411788724316)
XLA Ops:
  6.5 0.0 copy-start
  6.5 0.0 copy-start.5
  6.5 0.0 all-gather.3.cloned.1.call-start
  6.5 2.4 %shard_map.100 = (bf16[2,3,64,768]{3,2,1,0:T(8,128)(2,1)}, s32[32,32]{1,0:T(8,128)}, s32[4,128]{1,0:T(4,128)}) custom-call(s32[4,128]{1,0:T(4,128)} %bitcast.28, s32[4,128]{1,0:T(4,128)} %row_ref.1, bf16[2,64,768]{2,1,0:T(8,128)(2,1)} %gate_ref.1, bf16[2,64,768]{2,1,0:T(8,128)(2,1)} %up_ref.1, bf16[2,48,1024]{2,1,0:T(8,128)(2,1)} %down_ref.1), custom_call_target="tpu_custom_call" | custom-call | tf_op jit(solution)/shard_map/pallas_call | solution.py:238
  8.9 0.0 copy-start.1
  8.9 0.0 all-gather.3.cloned.1.call-update
  8.9 28.6 %all_to_all.33 = s32[32,1,32]{2,1,0:T(1,128)S(1)} all-to-all(s32[32,1,32]{2,1,0:T(1,128)} %bitcast.27), channel_id=1, replica_groups=mesh['tok'=32,'batch'=16] {'tok'}, dimensions={0} | all-to-all | bytes 8192 | tf_op jit(solution)/shard_map/all_to_all | solution.py:262
  37.5 0.1 copy.19
  37.6 0.1 copy.20
  37.7 0.1 copy.21
  37.8 13.0 %all_to_all.34 = s32[16,1,64]{2,1,0:T(1,128)S(1)} all-to-all(s32[16,1,64]{2,1,0:T(1,128)S(1)} %copy.21), channel_id=1, replica_groups=mesh['tok'=32,'batch'=16] {'batch'}, dimensions={0} | all-to-all | bytes 8192 | tf_op jit(solution)/shard_map/all_to_all | solution.py:264
  50.7 0.1 copy.22
  50.8 0.3 copy.23
  51.1 0.2 eq.15
  51.2 0.0 copy-done
  51.3 0.0 copy-start.2
  51.3 0.8 fusion
  52.1 1.0 reshape.36
  53.1 10.6 %all-to-all-start.2 = ((bf16[512,2,256]{2,1,0:T(2,128)(2,1)}), bf16[512,2,256]{2,1,0:T(2,128)(2,1)S(1)}, u32[]{:S(2)}, u32[]{:S(2)}) async-start(bf16[512,2,256]{2,1,0:T(2,128)(2,1)} %reshape.36), calls=%async_computation.2 | async-start | bytes 1048576 | tf_op jit(solution)/shard_map/all_to_all | solution.py:272
  63.7 0.0 copy-done.5
  63.7 0.2 copy.24
  63.9 35.9 %all-to-all-done.2 = bf16[512,2,256]{2,1,0:T(2,128)(2,1)S(1)} async-done(((bf16[512,2,256]{2,1,0:T(2,128)(2,1)}), bf16[512,2,256]{2,1,0:T(2,128)(2,1)S(1)}, u32[]{:S(2)}, u32[]{:S(2)}) %all-to-all-start.2) | async-done | bytes 524320 | tf_op jit(solution)/shard_map/all_to_all | solution.py:272
  99.8 0.2 reshape.37.answer_ref
  100.0 0.0 copy-done.1
  100.0 0.0 copy-done.3
  100.0 0.0 copy-done.4
  100.0 5.1 %shard_map.101 = bf16[32,8,1024]{2,1,0:T(8,128)(2,1)S(1)} custom-call(s32[4]{0:T(128)S(1)} %copy-done.4, bf16[1024,256]{1,0:T(8,128)(2,1)S(1)} %reshape.37.answer_ref, s32[4,128]{1,0:T(4,128)S(1)} %copy-done.3, bf16[256,1024]{1,0:T(8,128)(2,1)S(1)} %copy-done.1, bf16[8,128,64]{2,1,0:T(8,128)(2,1)S(1)} %bitcast.19), custom_call_target="tpu_custom_call" | custom-call | tf_op jit(solution)/shard_map/pallas_call | solution.py:92
  105.1 36.9 %all_to_all.35 = bf16[32,8,1024]{2,1,0:T(8,128)(2,1)S(1)} all-to-all(bf16[32,8,1024]{2,1,0:T(8,128)(2,1)S(1)} %shard_map.101), channel_id=1, replica_groups=mesh['tok'=32,'batch'=16] {'tok'}, dimensions={0} | all-to-all | bytes 1048576 | tf_op jit(solution)/shard_map/all_to_all | solution.py:276
  142.0 0.0 copy-done.2
  142.0 4.5 %shard_map.102 = bf16[32,2,2,16,128]{4,3,2,1,0:T(8,128)(2,1)S(1)} custom-call(bf16[256,1024]{1,0:T(8,128)(2,1)S(1)} %bitcast.18, f32[2,1024]{1,0:T(2,128)S(1)} %copy-done.2, bf16[16,2,3,64,768]{4,3,2,1,0:T(8,128)(2,1)} %bitcast.20), custom_call_target="tpu_custom_call" | custom-call | tf_op jit(solution)/shard_map/pallas_call | solution.py:169
  146.5 37.0 %all_to_all.36 = bf16[32,2,2,16,128]{4,3,2,1,0:T(8,128)(2,1)S(1)} all-to-all(bf16[32,2,2,16,128]{4,3,2,1,0:T(8,128)(2,1)S(1)} %shard_map.102), channel_id=1, replica_groups=mesh['tok'=32,'batch'=16] {'tok'}, dimensions={0} | all-to-all | bytes 1048576 | tf_op jit(solution)/shard_map/all_to_all | solution.py:280
  183.6 1.1 copy.26
  (4 shorter events, 0.0 us)
Async XLA Ops:
  6.5 44.7 %copy-start = (bf16[1024,256]{1,0:T(8,128)(2,1)S(1)}, bf16[1024,256]{1,0:T(8,128)(2,1)}, u32[]{:S(2)}) copy-start(bf16[1024,256]{1,0:T(8,128)(2,1)} %param.10) | copy-start | bytes 1572868
  6.5 57.1 %copy-start.5 = (bf16[64,1024]{1,0:T(8,128)(2,1)S(1)}, bf16[64,1024]{1,0:T(8,128)(2,1)}, u32[]{:S(2)}) copy-start(bf16[64,1024]{1,0:T(8,128)(2,1)} %param.15) | copy-start | bytes 393220
  6.5 135.5 %all-gather.3.cloned.1.call-start = ((), (), s32[]{:S(2)}) async-start(), calls=%async_computation.5 | async-start | bytes 10027008 | tf_op jit(solution)/shard_map/all_gather | solution.py:261
  8.9 91.1 %copy-start.1 = (bf16[256,1024]{1,0:T(8,128)(2,1)S(1)}, bf16[256,1024]{1,0:T(8,128)(2,1)}, u32[]{:S(2)}) copy-start(bf16[256,1024]{1,0:T(8,128)(2,1)} %w_in_ref.1) | copy-start | bytes 1572868
  8.9 91.1 %copy-start.3 = (s32[4,128]{1,0:T(4,128)S(1)}, s32[4,128]{1,0:T(4,128)}, u32[]{:S(2)}) copy-start(s32[4,128]{1,0:T(4,128)} %get-tuple-element.9.position_ref) | copy-start | bytes 6148
  8.9 91.1 %copy-start.4 = (s32[4]{0:T(128)S(1)}, s32[4]{0:T(128)}, u32[]{:S(2)}) copy-start(s32[4]{0:T(128)} %len_ref.1) | copy-start | bytes 52
  51.3 90.8 %copy-start.2 = (f32[2,1024]{1,0:T(2,128)S(1)}, f32[2,1024]{1,0:T(2,128)}, u32[]{:S(2)}) copy-start(f32[2,1024]{1,0:T(2,128)} %gain_ref.1) | copy-start | bytes 24580
  53.1 46.6 %all-to-all-start.2 = ((bf16[512,2,256]{2,1,0:T(2,128)(2,1)}), bf16[512,2,256]{2,1,0:T(2,128)(2,1)S(1)}, u32[]{:S(2)}, u32[]{:S(2)}) async-start(bf16[512,2,256]{2,1,0:T(2,128)(2,1)} %reshape.36), calls=%async_computation.2 | async-start | bytes 1048576 | tf_op jit(solution)/shard_map/all_to_all | solution.py:272
Sparse Core Ops, SparseCore 0:
  10.4 101.7 all-gather.2

commit v6 on v4

--- a/solution.py
+++ b/solution.py
@@ -116,9 +116,16 @@
     headsz = out_ref.shape[3]
     copies = []
     for token in range(tokens):
+        some = nparts // 2
         pieces = [
-            (weight_ref.at[:, token, :, :], gate_ref.at[token]),
-            (weight_ref.at[:, tokens + token, :, :], up_ref.at[token]),
+            (
+                weight_ref.at[pl.ds(first, some), kind * tokens + token, :, :],
+                into.at[token, pl.ds(first, some)],
+            )
+            for kind, into in enumerate((gate_ref, up_ref))
+            for first in (0, some)
+        ]
+        pieces += [
             (
                 weight_ref.at[:, 2 * tokens + token, pl.ds(0, down_rows), :],
                 down_ref.at[token, :, :, pl.ds(0, hidden_width)],
@@ -154,12 +161,14 @@
         wide = mixed[token * group : (token + 1) * group, :]
         scale = lax.rsqrt(jnp.mean(wide * wide, axis=-1, keepdims=True) + EPS)
         normed = (wide * scale * gain_ref[token : token + 1, :]).astype(jnp.bfloat16)
-        copies[token][0].wait()
+        for copy in copies[token][:2]:
+            copy.wait()
         gate = dot32(normed, gate_ref[token].reshape(width, hidden_width))
-        copies[token][1].wait()
+        for copy in copies[token][2:4]:
+            copy.wait()
         up_val = dot32(normed, up_ref[token].reshape(width, hidden_width))
         hidden = (gate / (1.0 + jnp.exp(-gate)) * up_val).astype(jnp.bfloat16)
-        for copy in copies[token][2:]:
+        for copy in copies[token][4:]:
             copy.wait()
         down = dot32(hidden, down_ref[token].reshape(hidden_width, width))
         summed = (wide + down).T.astype(jnp.bfloat16)
@@ -175,7 +184,7 @@
     nparts, _, part_rows, hidden_width = weights.shape
     down_rows = hidden_width // nparts
     nquery = ntok * tokens
-    pieces = 3 + down_rows // (part_rows - down_rows)
+    pieces = 5 + down_rows // (part_rows - down_rows)
     return pl.pallas_call(
         net_kernel,
         in_specs=[

time: 192 us -> 192 us (level)
  no operation moved by 1% of the time
where the time goes in v6:
time: 192 us; the launch traced here: 191 us
  blocking collectives  115 us (60%)
  waiting for transfers between devices  35.9 us (19%)
  between operations  13.5 us (7%)
  Pallas kernels  11.7 us (6%)
  starting transfers between devices  10.6 us (6%)
  local copies, waits for them, and re-layouts  3.28 us (2%)
    all_to_all x1, blocking collectives, shards(): back = lax.all_to_all(sent, 'tok', 0, 0, tiled=True)  37 us
    all_to_all x1, blocking collectives, shards(): mixed = lax.all_to_all(pooled, 'tok', 0, 0, tiled=True)  36.9 us
    all_to_all x1, waiting for transfers between devices, shards(): lax.all_to_all(served.reshape(devices, cap, emb), ('tok', 'batch'), 0, 0,...  35.9 us
    all_to_all x1, blocking collectives, shards(): asked = lax.all_to_all(request, 'tok', 0, 0, tiled=True)  28.6 us
    all_to_all x1, blocking collectives, shards(): asked = lax.all_to_all(asked, 'batch', 0, 0, tiled=True)  13 us
    all_to_all x1, starting transfers between devices, shards(): lax.all_to_all(served.reshape(devices, cap, emb), ('tok', 'batch'), 0, 0,...  10.6 us
    pallas_call x1, Pallas kernels, pool(): pl.pallas_call(pool_kernel, grid=(parts // INNER,), in_specs=[pl.BlockSpe...  5.1 us
    pallas_call x1, Pallas kernels, net(): pl.pallas_call(net_kernel, in_specs=[pl.BlockSpec(memory_space=pltpu.VMEM...  4.3 us
  transfers between devices with their start and end apart: 2, of which 1 were waited for; matrix products, arithmetic and copies ran while one was open for 2% of the time, Pallas kernels for 3%

profile of v6, /device:TPU:1, one launch (start us, length us, event | category | flops | bytes accessed | tf_op | source)
XLA Modules:
  0.0 191.3 jit_solution(15332941855160152946)
XLA Ops:
  6.5 0.0 copy-start
  6.5 0.0 copy-start.5
  6.5 0.0 all-gather.3.cloned.1.call-start
  6.5 2.4 %shard_map.100 = (bf16[6,64,768]{2,1,0:T(8,128)(2,1)}, s32[32,32]{1,0:T(8,128)}, s32[4,128]{1,0:T(4,128)}) custom-call(s32[4,128]{1,0:T(4,128)} %bitcast.28, s32[4,128]{1,0:T(4,128)} %row_ref.1, bf16[2,64,768]{2,1,0:T(8,128)(2,1)} %gate_ref.1, bf16[2,64,768]{2,1,0:T(8,128)(2,1)} %up_ref.1, bf16[2,48,1024]{2,1,0:T(8,128)(2,1)} %down_ref.1), custom_call_target="tpu_custom_call" | custom-call | tf_op jit(solution)/shard_map/pallas_call | solution.py:258
  8.9 0.0 copy-start.1
  8.9 0.0 all-gather.3.cloned.1.call-update
  8.9 28.6 %all_to_all.33 = s32[32,1,32]{2,1,0:T(1,128)S(1)} all-to-all(s32[32,1,32]{2,1,0:T(1,128)} %bitcast.27), channel_id=1, replica_groups=mesh['tok'=32,'batch'=16] {'tok'}, dimensions={0} | all-to-all | bytes 8192 | tf_op jit(solution)/shard_map/all_to_all | solution.py:282
  37.5 0.1 copy.19
  37.6 0.1 copy.20
  37.7 0.1 copy.21
  37.8 13.0 %all_to_all.34 = s32[16,1,64]{2,1,0:T(1,128)S(1)} all-to-all(s32[16,1,64]{2,1,0:T(1,128)S(1)} %copy.21), channel_id=1, replica_groups=mesh['tok'=32,'batch'=16] {'batch'}, dimensions={0} | all-to-all | bytes 8192 | tf_op jit(solution)/shard_map/all_to_all | solution.py:284
  50.7 0.1 copy.22
  50.8 0.3 copy.23
  51.1 0.2 eq.15
  51.2 0.0 copy-done
  51.3 0.0 copy-start.2
  51.3 0.8 fusion
  52.1 1.0 reshape.36
  53.1 10.6 %all-to-all-start.2 = ((bf16[512,2,256]{2,1,0:T(2,128)(2,1)}), bf16[512,2,256]{2,1,0:T(2,128)(2,1)S(1)}, u32[]{:S(2)}, u32[]{:S(2)}) async-start(bf16[512,2,256]{2,1,0:T(2,128)(2,1)} %reshape.36), calls=%async_computation.2 | async-start | bytes 1048576 | tf_op jit(solution)/shard_map/all_to_all | solution.py:292
  63.7 0.0 copy-done.5
  63.7 0.2 copy.24
  63.9 35.9 %all-to-all-done.2 = bf16[512,2,256]{2,1,0:T(2,128)(2,1)S(1)} async-done(((bf16[512,2,256]{2,1,0:T(2,128)(2,1)}), bf16[512,2,256]{2,1,0:T(2,128)(2,1)S(1)}, u32[]{:S(2)}, u32[]{:S(2)}) %all-to-all-start.2) | async-done | bytes 524320 | tf_op jit(solution)/shard_map/all_to_all | solution.py:292
  99.8 0.2 reshape.37.answer_ref
  100.0 0.0 copy-done.1
  100.0 0.0 copy-done.3
  100.0 0.0 copy-done.4
  100.0 5.1 %shard_map.101 = bf16[32,8,1024]{2,1,0:T(8,128)(2,1)S(1)} custom-call(s32[4]{0:T(128)S(1)} %copy-done.4, bf16[1024,256]{1,0:T(8,128)(2,1)S(1)} %reshape.37.answer_ref, s32[4,128]{1,0:T(4,128)S(1)} %copy-done.3, bf16[256,1024]{1,0:T(8,128)(2,1)S(1)} %copy-done.1, bf16[8,128,64]{2,1,0:T(8,128)(2,1)S(1)} %bitcast.19), custom_call_target="tpu_custom_call" | custom-call | tf_op jit(solution)/shard_map/pallas_call | solution.py:92
  105.1 36.9 %all_to_all.35 = bf16[32,8,1024]{2,1,0:T(8,128)(2,1)S(1)} all-to-all(bf16[32,8,1024]{2,1,0:T(8,128)(2,1)S(1)} %shard_map.101), channel_id=1, replica_groups=mesh['tok'=32,'batch'=16] {'tok'}, dimensions={0} | all-to-all | bytes 1048576 | tf_op jit(solution)/shard_map/all_to_all | solution.py:296
  142.0 0.0 copy-done.2
  142.0 4.3 %shard_map.102 = bf16[32,2,2,16,128]{4,3,2,1,0:T(8,128)(2,1)S(1)} custom-call(bf16[256,1024]{1,0:T(8,128)(2,1)S(1)} %bitcast.18, f32[2,1024]{1,0:T(2,128)S(1)} %copy-done.2, bf16[16,6,64,768]{3,2,1,0:T(8,128)(2,1)} %bitcast.20), custom_call_target="tpu_custom_call" | custom-call | tf_op jit(solution)/shard_map/pallas_call | solution.py:188
  146.3 37.0 %all_to_all.36 = bf16[32,2,2,16,128]{4,3,2,1,0:T(8,128)(2,1)S(1)} all-to-all(bf16[32,2,2,16,128]{4,3,2,1,0:T(8,128)(2,1)S(1)} %shard_map.102), channel_id=1, replica_groups=mesh['tok'=32,'batch'=16] {'tok'}, dimensions={0} | all-to-all | bytes 1048576 | tf_op jit(solution)/shard_map/all_to_all | solution.py:300
  183.4 1.1 copy.26
  (4 shorter events, 0.0 us)
Async XLA Ops:
  6.5 44.7 %copy-start = (bf16[1024,256]{1,0:T(8,128)(2,1)S(1)}, bf16[1024,256]{1,0:T(8,128)(2,1)}, u32[]{:S(2)}) copy-start(bf16[1024,256]{1,0:T(8,128)(2,1)} %param.10) | copy-start | bytes 1572868
  6.5 57.1 %copy-start.5 = (bf16[64,1024]{1,0:T(8,128)(2,1)S(1)}, bf16[64,1024]{1,0:T(8,128)(2,1)}, u32[]{:S(2)}) copy-start(bf16[64,1024]{1,0:T(8,128)(2,1)} %param.15) | copy-start | bytes 393220
  6.5 135.5 %all-gather.3.cloned.1.call-start = ((), (), s32[]{:S(2)}) async-start(), calls=%async_computation.5 | async-start | bytes 10027008 | tf_op jit(solution)/shard_map/all_gather | solution.py:281
  8.9 91.1 %copy-start.1 = (bf16[256,1024]{1,0:T(8,128)(2,1)S(1)}, bf16[256,1024]{1,0:T(8,128)(2,1)}, u32[]{:S(2)}) copy-start(bf16[256,1024]{1,0:T(8,128)(2,1)} %w_in_ref.1) | copy-start | bytes 1572868
  8.9 91.1 %copy-start.3 = (s32[4,128]{1,0:T(4,128)S(1)}, s32[4,128]{1,0:T(4,128)}, u32[]{:S(2)}) copy-start(s32[4,128]{1,0:T(4,128)} %get-tuple-element.9.position_ref) | copy-start | bytes 6148
  8.9 91.1 %copy-start.4 = (s32[4]{0:T(128)S(1)}, s32[4]{0:T(128)}, u32[]{:S(2)}) copy-start(s32[4]{0:T(128)} %len_ref.1) | copy-start | bytes 52
  51.3 90.8 %copy-start.2 = (f32[2,1024]{1,0:T(2,128)S(1)}, f32[2,1024]{1,0:T(2,128)}, u32[]{:S(2)}) copy-start(f32[2,1024]{1,0:T(2,128)} %gain_ref.1) | copy-start | bytes 24580
  53.1 46.6 %all-to-all-start.2 = ((bf16[512,2,256]{2,1,0:T(2,128)(2,1)}), bf16[512,2,256]{2,1,0:T(2,128)(2,1)S(1)}, u32[]{:S(2)}, u32[]{:S(2)}) async-start(bf16[512,2,256]{2,1,0:T(2,128)(2,1)} %reshape.36), calls=%async_computation.2 | async-start | bytes 1048576 | tf_op jit(solution)/shard_map/all_to_all | solution.py:292
Sparse Core Ops, SparseCore 0:
  10.4 101.7 all-gather.2
